TPU v7x, 128 devices: a whole 4x4x4 slice. The times are simulated.
128 devices in a mesh: res: 32 (over x, y_lo, z), seq: 4 (over y_hi, core).
Axes of the slice: x: 4, y: 4 (y_hi: 2, y_lo: 2; y = y_hi * 2 + y_lo), z: 4, core: 2. Of those that a mesh axis runs over, the one named last changes fastest.
Arguments:
- aligned_family_array: float32 [128, 768, 256], P('seq', 'res'), may hold values from -6 to 6
- couple_representation: float32 [768, 768, 128], P('res', 'seq'), may hold values from -6 to 6
- amino_real_flags: int32 [768], replicated, may hold values 0 or 1
- polymer_identity: int32 [768], replicated, may hold values from 0 to 3, as said below
- homolog_live_flags: int32 [128], replicated, may hold values 0 or 1
- projection_quartet_matrix: bfloat16 [256, 1024], replicated, may hold values from -0.8 to 0.8
- couple_shift_matrix: float32 [128, 8], replicated, may hold values from -0.5 to 0.5
- cross_polymer_score_shift: float32 [8], replicated, may hold values from -2 to 2
- mixing_exit_matrix: bfloat16 [256, 256], replicated, may hold values from -0.375 to 0.375
- factor_pair_matrices: bfloat16 [256, 64], replicated, may hold values from -0.375 to 0.375
- tensor_mean_matrix: float32 [1024, 128], replicated, may hold values from -1 to 1
Outputs:
- family_array_reweighted: float32 [128, 768, 256], P('seq', 'res')
- contact_grid_result: float32 [768, 768, 128], P('res', 'seq')
Inputs may be any that keep to these rules, and one draw needn't show every extreme that they name: `polymer_identity`: each chain is one run of consecutive residues; there are at most four chains.
All inputs are finite; a program needn't handle non-finite values.
Results may differ from a plain program's by a relative error of at most 0.0029.
Values may be sent and summed in bfloat16 or wider, within the bound.
A program may use at most 320 MiB of HBM per device.

v0:
```python
import jax
import jax.numpy as jnp
from jax import lax
from jax.sharding import PartitionSpec as P


def zscore_elements(value_rows):
    centre = jnp.mean(value_rows, axis=-1, keepdims=True)
    spread = jnp.mean((value_rows - centre) ** 2, axis=-1, keepdims=True)
    return (value_rows - centre) * lax.rsqrt(spread + 1e-05)


def on_device(
    aligned_family_array,
    couple_representation,
    amino_real_flags,
    polymer_identity,
    homolog_live_flags,
    projection_quartet_matrix,
    couple_shift_matrix,
    cross_polymer_score_shift,
    mixing_exit_matrix,
    factor_pair_matrices,
    tensor_mean_matrix,
):
    homolog_number, amino_number, embedding_dimension = aligned_family_array.shape
    heads = couple_shift_matrix.shape[1]
    feature_width = projection_quartet_matrix.shape[1] // 4
    head_dim = feature_width // heads
    opm_dim = factor_pair_matrices.shape[1] // 2
    residues = amino_real_flags.shape[0]
    res_start = lax.axis_index("res") * amino_number
    seq_start = lax.axis_index("seq") * homolog_number
    standardized_stack = zscore_elements(aligned_family_array).astype(jnp.bfloat16)
    projected = jnp.dot(
        standardized_stack.reshape(-1, embedding_dimension),
        projection_quartet_matrix,
        preferred_element_type=jnp.float32,
    )
    projected = projected.astype(jnp.bfloat16).reshape(
        homolog_number, amino_number, 4 * feature_width
    )
    query_rows = projected[:, :, :feature_width].reshape(
        homolog_number, amino_number, heads, head_dim
    )
    gate_values = projected[:, :, 3 * feature_width :].astype(jnp.float32)
    key_rows, value_rows = (
        lax.all_gather(
            projected[:, :, feature_width : 2 * feature_width], "res", axis=1, tiled=True
        ),
        lax.all_gather(
            projected[:, :, 2 * feature_width : 3 * feature_width], "res", axis=1, tiled=True
        ),
    )
    key_rows = key_rows.reshape(homolog_number, residues, heads, head_dim)
    value_rows = value_rows.reshape(homolog_number, residues, heads, head_dim)
    local_bias = jnp.einsum(
        "ijc,ch->hij",
        zscore_elements(couple_representation),
        couple_shift_matrix,
        precision=lax.Precision.HIGHEST,
    )
    bias = lax.all_gather(local_bias, "seq", axis=2, tiled=True)
    own_chain = lax.dynamic_slice_in_dim(polymer_identity, res_start, amino_number)
    differ = (own_chain[:, None] != polymer_identity[None, :]).astype(jnp.float32)
    bias = bias + cross_polymer_score_shift[:, None, None] * differ[None]
    scores = jnp.einsum("sihd,sjhd->shij", query_rows, key_rows, preferred_element_type=jnp.float32)
    scores = scores / jnp.sqrt(jnp.float32(head_dim)) + bias[None]
    scores = jnp.where(
        (amino_real_flags > 0)[None, None, None, :], scores, jnp.float32(-1000000000.0)
    )
    row_max = jnp.max(scores, axis=-1, keepdims=True)
    expo = jnp.exp(scores - row_max)
    weights = (expo / jnp.sum(expo, axis=-1, keepdims=True)).astype(jnp.bfloat16)
    attended = jnp.einsum(
        "shij,sjhd->sihd", weights, value_rows, preferred_element_type=jnp.float32
    )
    gated = (
        attended.reshape(homolog_number, amino_number, feature_width) * jax.nn.sigmoid(gate_values)
    ).astype(jnp.bfloat16)
    delta_accrued = jnp.dot(
        gated.reshape(-1, feature_width), mixing_exit_matrix, preferred_element_type=jnp.float32
    )
    existing_sequences = lax.dynamic_slice_in_dim(
        homolog_live_flags, seq_start, homolog_number
    ).astype(jnp.float32)
    family_array_reweighted = aligned_family_array + existing_sequences[
        :, None, None
    ] * delta_accrued.reshape(homolog_number, amino_number, embedding_dimension)
    res_live = amino_real_flags.astype(jnp.float32)
    own_live = lax.dynamic_slice_in_dim(res_live, res_start, amino_number)
    rescaled_other_operand_z = zscore_elements(family_array_reweighted).astype(jnp.bfloat16)
    factors = jnp.dot(
        rescaled_other_operand_z.reshape(-1, embedding_dimension),
        factor_pair_matrices,
        preferred_element_type=jnp.float32,
    )
    factors = (
        factors.reshape(homolog_number, amino_number, 2 * opm_dim)
        * (existing_sequences[:, None] * own_live[None, :])[:, :, None]
    )
    factors = factors.astype(jnp.bfloat16)
    left = factors[:, :, :opm_dim]
    right_all = lax.all_gather(factors[:, :, opm_dim:], "res", axis=1, tiled=True)
    col_count = residues // lax.axis_size("seq")
    col_start = lax.axis_index("seq") * col_count
    outer = jnp.einsum("sic,sje->jice", left, right_all, preferred_element_type=jnp.float32)
    outer = outer.reshape(lax.axis_size("seq") * col_count, amino_number, opm_dim * opm_dim)
    summed = lax.psum_scatter(
        jnp.einsum("jik,kz->jiz", outer, tensor_mean_matrix, precision=lax.Precision.HIGHEST),
        "seq",
        scatter_dimension=0,
        tiled=True,
    )
    col_live = lax.dynamic_slice_in_dim(res_live, col_start, col_count)
    live_rows = jnp.sum(homolog_live_flags.astype(jnp.float32))
    norm = jnp.maximum(live_rows * own_live[:, None] * col_live[None, :], 1.0)
    contact_grid_result = (
        couple_representation + jnp.transpose(summed, (1, 0, 2)) / norm[:, :, None]
    )
    return (family_array_reweighted, contact_grid_result)


def solution(mesh):
    in_specs = (
        P("seq", "res", None),
        P("res", "seq", None),
        P(),
        P(),
        P(),
        P(),
        P(),
        P(),
        P(),
        P(),
        P(),
    )
    out_specs = (P("seq", "res", None), P("res", "seq", None))
    return jax.shard_map(
        on_device, mesh=mesh, in_specs=in_specs, out_specs=out_specs, check_vma=False
    )
```

profile of v0, /device:TPU:0, one launch (start us, length us, event | category | flops | bytes accessed | tf_op | source)
XLA Modules:
  0.0 918.7 jit_solution(16719314137762113983)
XLA Ops:
  7.2 1.5 reduce_sum.72
  8.7 1.4 multiply_reduce_fusion.2
  10.2 1.4 multiply_convert_fusion.2
  11.6 1.6 convolution_convert_fusion
  13.2 1.1 copy-done.4
  14.4 1.0 fusion.41
  15.4 0.7 all-gather.4.cloned.1.call-update
  16.2 0.9 reduce_sum.74
  17.1 1.7 multiply_reduce_fusion
  18.9 5.0 fusion.25
  24.3 63.8 %all_gather.14 = f32[8,24,768]{1,0,2:T(8,128)} all-gather(f32[8,24,192]{1,0,2:T(8,128)S(1)} %copy.40), channel_id=1, replica_groups=mesh['res'=32,'seq'=4] {'seq'}, dimensions={2}, use_global_device_ids=true | all-gather | bytes 737280 | tf_op jit(solution)/shard_map/all_gather | solution.py:63
  88.0 2.4 copy.41
  91.2 0.6 convert_reduce_fusion
  91.9 1.3 broadcast_multiply_fusion.4
  93.4 108.0 %all-gather.6.cloned.1.call-done = bf16[32,768,256]{2,1,0:T(8,128)(2,1)} async-done(((bf16[32,24,256]{2,1,0:T(8,128)(2,1)}), bf16[32,768,256]{2,1,0:T(8,128)(2,1)}) %all-gather.6.cloned.1.call-update) | async-done | bytes 12582928 | tf_op jit(solution)/shard_map/all_gather | solution.py:48
  201.4 16.7 %copy.38 = bf16[32,768,256]{1,2,0:T(8,128)(2,1)} copy(bf16[32,768,256]{2,1,0:T(8,128)(2,1)} %all-gather.6.cloned.1.call-done) | data formatting | bytes 25165824 | tf_op jit(solution)/shard_map/all_gather | solution.py:48
  218.1 13.6 %fusion.43 = (f32[32,8,24]{2,1,0:T(8,128)S(1)}, f32[32,8,24,768]{3,2,1,0:T(8,128)}) fusion(f32[8,24,768]{2,1,0:T(8,128)S(1)} %multiply_add_fusion, pred[768]{0:T(1024)(128)(4,1)S(1)} %broadcast_compare_fusion, bf16[32,768,8,32]{1,3,2,0:T(8,128)(2,1)} %bitcast.42, bf16[32,24,8,32]{3,2,1,0:T(8,128)(2,1)S(1)} %reshape.162), kind=kOutput, calls=%fused_computation.64 | convolution fusion | flops 325583616 | bytes 32465664 | tf_op jit(solution)/shard_map/sub | solution.py:73
  231.7 147.8 %all-gather.4.cloned.1.call-done = bf16[32,768,256]{2,1,0:T(8,128)(2,1)} async-done(((bf16[32,24,256]{2,1,0:T(8,128)(2,1)}), bf16[32,768,256]{2,1,0:T(8,128)(2,1)}) %all-gather.4.cloned.1.call-update) | async-done | bytes 12582928 | tf_op jit(solution)/shard_map/all_gather | solution.py:51
  379.5 16.7 %copy.37 = bf16[32,768,256]{1,2,0:T(8,128)(2,1)} copy(bf16[32,768,256]{2,1,0:T(8,128)(2,1)} %all-gather.4.cloned.1.call-done) | data formatting | bytes 25165824 | tf_op jit(solution)/shard_map/all_gather | solution.py:51
  396.1 13.6 %fusion.13 = f32[32,24,8,32]{3,1,2,0:T(8,128)} fusion(bf16[32,768,8,32]{1,3,2,0:T(8,128)(2,1)} %bitcast.43, f32[32,8,24,768]{3,2,1,0:T(8,128)} %get-tuple-element.10, f32[32,8,24]{2,1,0:T(8,128)S(1)} %get-tuple-element.9), kind=kOutput, calls=%fused_computation.18 | convolution fusion | flops 311427072 | bytes 32268288 | tf_op jit(solution)/shard_map/shij,sjhd->sihd/dot_general | solution.py:75
  409.7 4.2 copy.42
  413.9 2.4 reshape.164
  416.3 1.5 fusion.48
  419.1 0.8 fusion.42
  420.4 159.5 %all-gather.8.cloned.1.call-done = bf16[32,768,32]{2,1,0:T(8,128)(2,1)} async-done(((bf16[32,24,32]{2,1,0:T(8,128)(2,1)}), bf16[32,768,32]{2,1,0:T(8,128)(2,1)}) %all-gather.8.cloned.1.call-update) | async-done | bytes 1572880 | tf_op jit(solution)/shard_map/all_gather | solution.py:104
  579.9 13.9 %copy.47 = bf16[32,768,32,1]{0,1,3,2:T(8,128)(2,1)} copy(bf16[32,768,32,1]{2,1,0,3:T(8,128)(2,1)} %bitcast.44) | data formatting | bytes 3145728 | tf_op jit(solution)/shard_map/all_gather | solution.py:104
  593.9 29.8 %convolution_bitcast_fusion = f32[768,24,32,32]{0,2,1,3:T(8,128)} fusion(bf16[32,768,32,1]{0,1,3,2:T(8,128)(2,1)} %copy.47, bf16[32,24,32]{0,2,1:T(8,128)(2,1)S(1)} %copy.44), kind=kOutput, calls=%fused_computation.1 | convolution fusion | flops 1207959552 | bytes 77119488 | tf_op jit(solution)/shard_map/sic,sje->jice/dot_general | solution.py:107
  623.6 75.2 %copy.45 = f32[768,24,32,32]{0,3,2,1:T(8,128)} copy(f32[768,24,32,32]{0,2,1,3:T(8,128)} %convolution_bitcast_fusion) | data formatting | bytes 150994944 | tf_op jit(solution)/shard_map/sic,sje->jice/transpose | solution.py:107
  698.8 124.2 %fusion.28 = f32[768,24,128]{2,0,1:T(8,128)} fusion(f32[768,24,1024]{0,2,1:T(8,128)} %bitcast.12, f32[1024,128]{1,0:T(8,128)S(1)} %copy-done), kind=kOutput, calls=%fused_computation.36 | convolution fusion | flops 28991029248 | bytes 85458944 | tf_op jit(solution)/shard_map/jik,kz->jiz/dot_general | solution.py:110
  823.1 0.9 dynamic_slice.15
  824.1 84.7 %reduce-scatter.2.cloned.1.call-done = f32[192,24,128]{2,0,1:T(8,128)} async-done(((f32[768,24,128]{2,0,1:T(8,128)}), f32[192,24,128]{2,0,1:T(8,128)}) %reduce-scatter.2.cloned.1.call-update) | async-done | bytes 2359312 | tf_op jit(solution)/shard_map/reduce_scatter | solution.py:109
  908.8 3.1 fusion.7
  (54 shorter events, 3.4 us)
Async XLA Ops:
  7.2 691.6 %copy-start = (f32[1024,128]{1,0:T(8,128)S(1)}, f32[1024,128]{1,0:T(8,128)}, u32[]{:S(2)}) copy-start(f32[1024,128]{1,0:T(8,128)} %param.21) | copy-start | bytes 1572868
  7.2 9.0 copy-start.1
  7.2 194.2 %all-gather.6.cloned.1.call-start = ((), (), s32[]{:S(2)}) async-start(), calls=%async_computation.2 | async-start | bytes 12976128 | tf_op jit(solution)/shard_map/all_gather | solution.py:48
  8.7 10.1 %copy-start.9 = (f32[128,8]{0,1:T(8,128)S(1)}, f32[128,8]{0,1:T(8,128)}, u32[]{:S(2)}) copy-start(f32[128,8]{0,1:T(8,128)} %param.17) | copy-start | bytes 12292
  13.2 1.1 copy-start.4
  15.4 364.1 %all-gather.4.cloned.1.call-start = ((), (), s32[]{:S(2)}) async-start(), calls=%async_computation.1 | async-start | bytes 12976128 | tf_op jit(solution)/shard_map/all_gather | solution.py:51
  16.1 563.8 %all-gather.8.cloned.1.call-start = ((), (), s32[]{:S(2)}) async-start(), calls=%async_computation.3 | async-start | bytes 6488064 | tf_op jit(solution)/shard_map/all_gather | solution.py:104
  18.8 72.2 %copy-start.7 = (s32[768]{0:T(1024)S(1)}, s32[768]{0:T(1024)}, u32[]{:S(2)}) copy-start(s32[768]{0:T(1024)} %param.13) | copy-start | bytes 9220
  18.9 72.2 %copy-start.10 = (s32[768]{0:T(1024)S(1)}, s32[768]{0:T(1024)}, u32[]{:S(2)}) copy-start(s32[768]{0:T(1024)} %param.14) | copy-start | bytes 9220
  18.9 72.3 %copy-start.14 = (s32[128]{0:T(128)S(1)}, s32[128]{0:T(128)}, u32[]{:S(2)}) copy-start(s32[128]{0:T(128)} %param.15) | copy-start | bytes 1540
  18.9 74.3 %copy-start.12 = (f32[8]{0:T(128)S(1)}, f32[8]{0:T(128)}, u32[]{:S(2)}) copy-start(f32[8]{0:T(128)} %param.18) | copy-start | bytes 100
  91.1 2.1 copy-start.8
  409.7 6.6 copy-start.3
  409.7 6.6 copy-start.13
  413.9 4.8 copy-start.6
  417.8 0.9 copy-start.5
  420.0 488.9 %reduce-scatter.2.cloned.1.call-start = ((), (), s32[]{:S(2)}) async-start(), calls=%async_computation.4 | async-start | bytes 11796480 | tf_op jit(solution)/shard_map/reduce_scatter | solution.py:109
  823.1 0.9 copy-start.11
  823.1 85.8 %copy-start.2 = (f32[24,192,128]{2,1,0:T(8,128)S(1)}, f32[24,192,128]{2,1,0:T(8,128)}, u32[]{:S(2)}) copy-start(f32[24,192,128]{2,1,0:T(8,128)} %param.12) | copy-start | bytes 7077892
Sparse Core Ops, SparseCore 0:
  15.5 185.8 all-gather.5
  203.0 176.3 all-gather.3
  420.1 159.7 all-gather.7
  823.2 85.5 reduce-scatter.1
where the time goes:
time: 924 us; the launch traced here: 919 us
  waiting for transfers between devices  501 us (54%)
  matrix products  190 us (21%)
  local copies, waits for them, and re-layouts  137 us (15%)
  blocking collectives  63.8 us (7%)
  between operations  14.3 us (2%)
  other arithmetic  12.7 us (1%)
    all_gather x1, waiting for transfers between devices, on_device(): lax.all_gather(factors[:, :, opm_dim:], 'res', axis=1, tiled=True)  160 us
    all_gather x1, waiting for transfers between devices, on_device(): lax.all_gather(projected[:, :, 2 * feature_width:3 * feature_width], 'res...  148 us
    dot_general x1, matrix products, on_device(): jnp.einsum('jik,kz->jiz', outer, tensor_mean_matrix, precision=lax.Precis...  124 us
    all_gather x1, waiting for transfers between devices, on_device(): lax.all_gather(projected[:, :, feature_width:2 * feature_width], 'res', a...  108 us
    reduce_scatter x1, waiting for transfers between devices, on_device(): lax.psum_scatter(jnp.einsum('jik,kz->jiz', outer, tensor_mean_matrix, pre...  84.7 us
    transpose x1, local copies, waits for them, and re-layouts, on_device(): jnp.einsum('sic,sje->jice', left, right_all, preferred_element_type=jnp.f...  75.2 us
    all_gather x1, blocking collectives, on_device(): bias = lax.all_gather(local_bias, 'seq', axis=2, tiled=True)  63.8 us
    dot_general x1, matrix products, on_device(): jnp.einsum('sic,sje->jice', left, right_all, preferred_element_type=jnp.f...  29.8 us
  transfers between devices with their start and end apart: 4, of which 4 were waited for; matrix products, arithmetic and copies ran while one was open for 5% of the time, Pallas kernels for 0%

commit v1 on v0

v1 whole, which is shorter than its diff:
```python
import functools
import math

import jax
import jax.numpy as jnp
from jax import lax
from jax.experimental import pallas as pl
from jax.experimental.pallas import tpu as pltpu
from jax.sharding import PartitionSpec as P

MESH = pl.DeviceIdType.MESH
F32 = jnp.float32
BF16 = jnp.bfloat16
LOG2E = math.log2(math.e)
VMEM_LIMIT = 56 * 1024 * 1024

N_RES, N_SEQ = 32, 4
S_LOC, I_LOC, J_LOC = 32, 24, 192
CM, CZ, HEADS, HD, OPM = 256, 128, 8, 32, 32
RES = 768
GROUPS = 4
ROWS_PER = 8


def lane_iota(shape):
    return lax.broadcasted_iota(jnp.int32, shape, len(shape) - 1)


def layer_norm(x):
    centre = jnp.mean(x, axis=-1, keepdims=True)
    d = x - centre
    spread = jnp.mean(d * d, axis=-1, keepdims=True)
    return d * lax.rsqrt(spread + 1e-05)


def project_kernel(msa, w, pair, wshift, qkvg, bias):
    s = lax.axis_index("seq")
    normed = layer_norm(msa[...].reshape(S_LOC * I_LOC, CM)).astype(BF16)
    lane = lane_iota((CM, 128))
    lane_o = lane_iota((S_LOC * I_LOC, 128))
    scale = jnp.where(lane_o < HD, F32(LOG2E / math.sqrt(HD)), F32(1.0))
    for h in range(HEADS):
        wh = None
        for part in range(4):
            col = part * 256 + (h // 4) * 128
            piece = w[:, col : col + 128].astype(F32)
            shift = (part * 32 - (h % 4) * 32) % 128
            if shift:
                piece = pltpu.roll(piece, shift, 1)
            wh = piece if wh is None else jnp.where(lane >= part * 32, piece, wh)
        out = jnp.dot(normed, wh.astype(BF16), preferred_element_type=F32) * scale
        qkvg[h] = out.astype(BF16).reshape(GROUPS, ROWS_PER, I_LOC, 128)
    odd = s % 2
    chunk = 4
    for i0 in range(0, I_LOC, chunk):
        z = layer_norm(pair[i0 : i0 + chunk].reshape(chunk * J_LOC, CZ))
        b = lax.dot_general(
            wshift[...],
            z,
            (((0,), (1,)), ((), ())),
            precision=lax.Precision.HIGHEST,
            preferred_element_type=F32,
        )
        for i in range(chunk):
            row = b[:, i * J_LOC : (i + 1) * J_LOC]
            bias[i0 + i] = row


def project(msa, w, pair, wshift):
    return pl.pallas_call(
        project_kernel,
        out_shape=(
            jax.ShapeDtypeStruct((HEADS, GROUPS, ROWS_PER, I_LOC, 128), BF16),
            jax.ShapeDtypeStruct((I_LOC, HEADS, J_LOC), F32),
        ),
        in_specs=[pl.BlockSpec(memory_space=pltpu.VMEM)] * 4,
        out_specs=(pl.BlockSpec(memory_space=pltpu.VMEM),) * 2,
        compiler_params=pltpu.CompilerParams(vmem_limit_bytes=VMEM_LIMIT),
        name="project",
    )(msa, w, pair, wshift)


def offset(k, r):
    kk = lax.rem(k * 11, N_RES)
    x = lax.rem(lax.div(r, 8) + lax.div(kk, 8), 4)
    y = lax.rem(lax.div(r, 4) + lax.div(kk, 4), 2)
    z = lax.rem(r + kk, 4)
    return x * 8 + y * 4 + z


def attend_kernel(
    qkvg, bias_in, poly_col, poly_row, amino_col, amino_row, shifts,
    back,
    recv, b1, br, bias, acc, ret,
    ss, rs, s1, r1, s2, r2, s3, r3, sb, rb, loc,
):
    r, s = lax.axis_index("res"), lax.axis_index("seq")
    h, z = lax.div(r, 4), lax.rem(r, 4)
    s_y = lax.rem(s + 2, 4)
    s_c = s + 1 - 2 * lax.rem(s, 2)

    def remote(src, dst, a, b, d, q):
        return pltpu.make_async_remote_copy(
            src_ref=src, dst_ref=dst, send_sem=a, recv_sem=b, device_id=(d, q), device_id_type=MESH
        )

    barrier = pltpu.get_barrier_semaphore()

    def greet(k, c):
        pl.semaphore_signal(barrier, inc=1, device_id=(offset(k, r), s), device_id_type=MESH)
        return c

    lax.fori_loop(1, N_RES, greet, 0)

    def greet_y(k, c):
        pl.semaphore_signal(barrier, inc=1, device_id=(h * 4 + k, s_y), device_id_type=MESH)
        return c

    lax.fori_loop(0, 4, greet_y, 0)
    pl.semaphore_signal(barrier, inc=1, device_id=(r, s_c), device_id_type=MESH)
    own = pltpu.make_async_copy(qkvg.at[r], recv.at[r], loc.at[0])
    own.start()
    own1 = pltpu.make_async_copy(bias_in.at[h], b1.at[h], loc.at[1])
    own1.start()
    pl.semaphore_wait(barrier, 36)

    def send1(k, c):
        hh = lax.rem(h + k, 8)
        remote(bias_in.at[hh], b1.at[h], s1.at[hh], r1.at[h], hh * 4 + z, s).start()
        return c

    lax.fori_loop(1, 8, send1, 0)

    def send(k, c):
        d = offset(k, r)
        remote(qkvg.at[d], recv.at[r], ss.at[d], rs.at[r], d, s).start()
        return c

    lax.fori_loop(1, N_RES, send, 0)

    def wait1(k, c):
        hh = lax.rem(h + k, 8)
        cp = remote(bias_in.at[hh], b1.at[hh], s1.at[hh], r1.at[hh], hh * 4 + z, s)
        cp.wait_send()
        cp.wait_recv()
        return c

    lax.fori_loop(1, 8, wait1, 0)
    own1.wait()
    own2 = pltpu.make_async_copy(b1, br.at[s, z], loc.at[2])
    own2.start()

    def send2(k, c):
        zz = lax.rem(z + k, 4)
        q = lax.rem(s + 2 * lax.div(k, 4), 4)
        remote(b1, br.at[s, z], s2.at[k], r2.at[lax.div(s, 2) * 4 + z], h * 4 + zz, q).start()
        return c

    lax.fori_loop(1, 8, send2, 0)

    def wait2(k, c):
        zz = lax.rem(z + k, 4)
        q = lax.rem(s + 2 * lax.div(k, 4), 4)
        cp = remote(b1, br.at[q, zz], s2.at[k], r2.at[lax.div(q, 2) * 4 + zz], h * 4 + zz, q)
        cp.wait_send()
        cp.wait_recv()
        return c

    lax.fori_loop(1, 8, wait2, 0)
    own2.wait()
    for t in range(2):
        q = lax.rem(s + 2 * t, 4)
        remote(br.at[q], br.at[q], s3.at[lax.div(q, 2)], r3.at[lax.div(q, 2)], r, s_c).start()

    def wait_in(k, c):
        d = offset(k, r)
        cp = remote(qkvg.at[d], recv.at[d], ss.at[d], rs.at[d], d, s)
        cp.wait_send()
        cp.wait_recv()
        return c

    lax.fori_loop(1, N_RES, wait_in, 0)
    own.wait()
    for t in range(2):
        q = lax.rem(s + 2 * t, 4)
        qc = q + 1 - 2 * lax.rem(q, 2)
        cp = remote(br.at[qc], br.at[qc], s3.at[lax.div(q, 2)], r3.at[lax.div(q, 2)], r, s_c)
        cp.wait_send()
        cp.wait_recv()

    shift = shifts[h]
    lane24 = lane_iota((I_LOC, 128))

    def build(k, c):
        zz, hh = lax.rem(k, 4), lax.div(k, 4)
        row = pl.multiple_of(k * I_LOC, 8)
        mine = poly_col[pl.ds(row, I_LOC), :]
        t = [br[q, zz, hh].astype(F32) for q in range(4)]
        tiles = [
            t[0][:, :128],
            jnp.where(lane24 < 64, t[0][:, 128:], t[1][:, :128]),
            t[1][:, 128:],
            t[2][:, :128],
            jnp.where(lane24 < 64, t[2][:, 128:], t[3][:, :128]),
            t[3][:, 128:],
        ]
        for n in range(6):
            cols = slice(n * 128, (n + 1) * 128)
            full = tiles[n] + jnp.where(mine != poly_row[:, cols], shift, F32(0.0))
            full = jnp.where(amino_row[:, cols] > 0, full * F32(LOG2E), F32(-1e9))
            bias[pl.ds(row, I_LOC), cols] = full
        return c

    lax.fori_loop(0, N_RES, build, 0)
    acc[...] = jnp.zeros_like(acc)
    lane = lane_iota((RES, 128))
    alive = amino_col[...] > 0

    def one_row(rr, c):
        x = recv[:, rr].astype(F32).reshape(RES, 128)
        xq = jnp.where(lane < HD, x, F32(0.0)).astype(BF16)
        turned = pltpu.roll(x, 96, 1)
        xk = jnp.where(alive, turned, F32(0.0)).astype(BF16)
        xv = jnp.where((lane >= 64) & (lane < 96), x, F32(1.0)).astype(BF16)
        gate = jax.nn.sigmoid(turned)
        slot = lax.rem(rr, 4) * HD
        for q0 in range(0, RES, 256):
            rows = slice(q0, q0 + 256)
            sc = lax.dot_general(
                xq[rows], xk, (((1,), (1,)), ((), ())), preferred_element_type=F32
            )
            sc = sc + bias[rows, :]
            m = jnp.max(sc, axis=-1, keepdims=True)
            p = jnp.exp2(sc - m).astype(BF16)
            o = jnp.dot(p, xv, preferred_element_type=F32)
            o = o / pltpu.roll(o, 64, 1) * gate[rows]
            o = pltpu.roll(o, lax.rem(slot + 64, 128), 1)
            ln = lane[rows]
            keep = (ln >= slot) & (ln < slot + HD)
            acc[lax.div(rr, 4), rows, :] += jnp.where(keep, o, F32(0.0))
        return c

    lax.fori_loop(0, ROWS_PER, one_row, 0)
    for half in range(2):
        ret[:, half] = acc[half].reshape(N_RES, I_LOC, 128).astype(BF16)

    ownb = pltpu.make_async_copy(ret.at[r], back.at[r], loc.at[3])
    ownb.start()

    def send_back(k, c):
        d = offset(k, r)
        remote(ret.at[d], back.at[r], sb.at[d], rb.at[r], d, s).start()
        return c

    lax.fori_loop(1, N_RES, send_back, 0)

    def wait_back(k, c):
        d = offset(k, r)
        cp = remote(ret.at[d], back.at[d], sb.at[d], rb.at[d], d, s)
        cp.wait_send()
        cp.wait_recv()
        return c

    lax.fori_loop(1, N_RES, wait_back, 0)
    ownb.wait()


def attend(qkvg, bias_in, poly, amino, shifts):
    dma = pltpu.SemaphoreType.DMA
    vm = pl.BlockSpec(memory_space=pltpu.VMEM)
    return pl.pallas_call(
        attend_kernel,
        out_shape=jax.ShapeDtypeStruct((N_RES, 2, I_LOC, 128), BF16),
        in_specs=[vm] * 6 + [pl.BlockSpec(memory_space=pltpu.SMEM)],
        out_specs=vm,
        scratch_shapes=[
            pltpu.VMEM((N_RES, ROWS_PER, I_LOC, 128), BF16),
            pltpu.VMEM((HEADS, I_LOC, 256), BF16),
            pltpu.VMEM((N_SEQ, 4, HEADS, I_LOC, 256), BF16),
            pltpu.VMEM((RES, RES), F32),
            pltpu.VMEM((2, RES, 128), F32),
            pltpu.VMEM((N_RES, 2, I_LOC, 128), BF16),
            dma((N_RES,)), dma((N_RES,)), dma((8,)), dma((8,)), dma((8,)), dma((8,)),
            dma((2,)), dma((2,)), dma((N_RES,)), dma((N_RES,)), dma((4,)),
        ],
        compiler_params=pltpu.CompilerParams(
            collective_id=0, has_side_effects=True, vmem_limit_bytes=VMEM_LIMIT
        ),
        name="attend",
    )(qkvg, bias_in, poly[:, None], poly[None, :], amino[:, None], amino[None, :], shifts)


J_CHUNK = 4


def outer_kernel(
    back, msa, pair, wmix, wfac, tmat, amino_col, live,
    family, contact,
    bd_mix, fac, tr, lbuf, rbuf, lall, rall, bd, tcat, lhs, amat,
    sl, rl, sr, rr_sem, loc,
):
    r, s = lax.axis_index("res"), lax.axis_index("seq")
    b, mine = lax.div(r, 8), lax.rem(r, 8) * 4 + s
    holds = b == s

    def remote(src, dst, a, bb, d, q):
        return pltpu.make_async_remote_copy(
            src_ref=src, dst_ref=dst, send_sem=a, recv_sem=bb, device_id=(d, q), device_id_type=MESH
        )

    def source(k):
        return 8 * s + lax.div(k, 4), lax.rem(k, 4)

    barrier = pltpu.get_barrier_semaphore()

    def greet(k, c):
        rr, q = source(k)

        @pl.when(jnp.logical_or(rr != r, q != s))
        def _():
            pl.semaphore_signal(barrier, inc=1, device_id=(rr, q), device_id_type=MESH)

        return c

    lax.fori_loop(0, N_RES, greet, 0)

    def greet_seq(k, c):
        pl.semaphore_signal(barrier, inc=1, device_id=(r, lax.rem(s + k, 4)), device_id_type=MESH)
        return c

    lax.fori_loop(1, N_SEQ, greet_seq, 0)

    bd_mix[...] = jnp.zeros_like(bd_mix)
    for h in range(HEADS):
        for k in range(4):
            bd_mix[h * 128 + k * 32 : h * 128 + (k + 1) * 32, k * CM : (k + 1) * CM] = wmix[
                h * HD : (h + 1) * HD, :
            ]
    gated = jnp.concatenate(
        [back[4 * h : 4 * h + 4].astype(F32).reshape(8 * I_LOC, 128) for h in range(HEADS)], axis=1
    ).astype(BF16)
    own_live = amino_col[pl.ds(pl.multiple_of(r * I_LOC, 8), I_LOC), :].astype(F32)
    for k in range(4):
        delta = jnp.dot(
            gated, bd_mix[:, k * CM : (k + 1) * CM], preferred_element_type=F32
        ).reshape(8, I_LOC, CM)
        for g in range(8):
            row = g * 4 + k
            on = live[s * S_LOC + row].astype(F32)
            fam = msa[row] + on * delta[g]
            family[row] = fam
            f = jnp.dot(layer_norm(fam).astype(BF16), wfac[...], preferred_element_type=F32)
            fac[row * I_LOC : (row + 1) * I_LOC, :] = jnp.concatenate(
                [f * (on * own_live), jnp.zeros((I_LOC, 64), F32)], axis=1
            )
    lane32 = lane_iota((S_LOC, 128))
    for i0 in range(0, I_LOC, 4):
        tile = jnp.zeros((S_LOC, 128), F32)
        for k in range(4):
            i = i0 + k
            f = fac[pl.ds(i, S_LOC, stride=I_LOC), :]
            moved = pltpu.roll(f, k * 32, 1) if k else f
            tile = jnp.where((lane32 >= k * 32) & (lane32 < (k + 1) * 32), moved, tile)
            ft = jnp.transpose(f, (1, 0))[OPM : 2 * OPM, :]
            tr[i * OPM : (i + 1) * OPM, :] = jnp.concatenate(
                [ft, jnp.zeros((OPM, 128 - S_LOC), F32)], axis=1
            )
        lbuf[:, i0 * 32 : (i0 + 4) * 32] = tile.astype(BF16)
    lane24 = lane_iota((I_LOC, 128))
    for e0 in range(0, OPM, 4):
        tile = tr[pl.ds(e0, I_LOC, stride=OPM), :]
        for k in range(1, 4):
            moved = pltpu.roll(tr[pl.ds(e0 + k, I_LOC, stride=OPM), :], k * 32, 1)
            tile = jnp.where((lane24 >= k * 32) & (lane24 < (k + 1) * 32), moved, tile)
        rbuf[:, e0 * 32 : (e0 + 4) * 32] = tile.astype(BF16)

    pl.semaphore_wait(barrier, N_RES - holds.astype(jnp.int32) + 3)

    def send_left(k, c):
        q = lax.rem(s + k, 4)
        remote(lbuf, lall.at[s], sl.at[q], rl.at[s], r, q).start()
        return c

    lax.fori_loop(1, N_SEQ, send_left, 0)

    def send_right(k, c):
        d = offset(k, r)

        @pl.when(jnp.logical_or(k != 0, jnp.logical_not(holds)))
        def _():
            remote(rbuf, rall.at[mine], sr.at[d], rr_sem.at[mine], d, b).start()

        return c

    lax.fori_loop(0, N_RES, send_right, 0)
    ownl = pltpu.make_async_copy(lbuf, lall.at[s], loc.at[0])
    ownl.start()

    @pl.when(holds)
    def _():
        cp = pltpu.make_async_copy(rbuf, rall.at[mine], loc.at[1])
        cp.start()
        cp.wait()

    for e in range(OPM):
        t = tmat[pl.ds(e, OPM, stride=OPM), :]
        head = t.astype(BF16)
        tcat[e * 32 : (e + 1) * 32, 0:128] = head
        tcat[e * 32 : (e + 1) * 32, 128:256] = (t - head.astype(F32)).astype(BF16)

    def wait_left(k, c):
        q = lax.rem(s + k, 4)
        cp = remote(lbuf, lall.at[q], sl.at[q], rl.at[q], r, q)
        cp.wait_send()
        cp.wait_recv()
        return c

    lax.fori_loop(1, N_SEQ, wait_left, 0)
    ownl.wait()
    sel_r = lax.broadcasted_iota(jnp.int32, (128, 512), 0)
    sel_c = lax.broadcasted_iota(jnp.int32, (128, 512), 1)
    same = (lax.div(sel_r, 32) == lax.div(sel_c, 128)) & (lax.rem(sel_r, 32) == lax.rem(sel_c, 32))
    sel = jnp.where(same, F32(1.0), F32(0.0)).astype(BF16)
    for i0 in range(0, I_LOC, 4):
        for q in range(N_SEQ):
            rep = jnp.dot(lall[q, :, i0 * 32 : (i0 + 4) * 32], sel, preferred_element_type=F32)
            for k in range(4):
                i = i0 + k
                piece = rep[:, k * 128 : (k + 1) * 128]
                for e in range(4):
                    keep = (lane32 >= e * 32) & (lane32 < (e + 1) * 32)
                    bd[
                        i // 2,
                        q * 128 + e * 32 : q * 128 + (e + 1) * 32,
                        (i % 2) * 128 : (i % 2 + 1) * 128,
                    ] = jnp.where(keep, piece, F32(0.0)).astype(BF16)

    count = lax.fori_loop(
        0, 128, lambda k, c: c + live[k], jnp.int32(0)
    ).astype(F32)
    inv = 1.0 / jnp.maximum(jnp.full((1, 128), count, F32), 1.0)

    def wait_right(k, c):
        rr, q = source(k)

        @pl.when(jnp.logical_or(rr != r, q != s))
        def _():
            remote(rbuf, rall.at[k], sr.at[k], rr_sem.at[k], rr, q).wait_recv()

        return c

    jc = J_CHUNK * I_LOC
    for c0 in range(0, 8, J_CHUNK):
        lax.fori_loop(4 * c0, 4 * (c0 + J_CHUNK), wait_right, 0)
        for q in range(N_SEQ):
            for g in range(8):
                cols = slice(g * 128, (g + 1) * 128)
                rows = jnp.concatenate(
                    [rall[4 * (c0 + t) + q, :, cols].astype(F32) for t in range(J_CHUNK)], axis=0
                )
                lhs[g * jc : (g + 1) * jc, q * 128 : (q + 1) * 128] = rows.astype(BF16)

        def pair_of(p, c):
            a = jnp.dot(lhs[...], bd[p], preferred_element_type=F32).astype(BF16)
            for half in range(2):
                for g in range(8):
                    amat[2 * p + half, :, g * 128 : (g + 1) * 128] = a[
                        g * jc : (g + 1) * jc, half * 128 : (half + 1) * 128
                    ]
            return c

        lax.fori_loop(0, I_LOC // 2, pair_of, 0)

        def finish(p, c):
            am = amat[pl.ds(4 * p, 4)].reshape(4 * jc, 1024)
            o = jnp.dot(am, tcat[...], preferred_element_type=F32)
            o = (o[:, :128] + o[:, 128:]) * inv
            where = (pl.ds(4 * p, 4), pl.ds(c0 * I_LOC, jc))
            contact[where] = pair[where] + o.reshape(4, jc, CZ)
            return c

        lax.fori_loop(0, I_LOC // 4, finish, 0)

    def wait_sent(k, c):
        @pl.when(jnp.logical_or(k != r, jnp.logical_not(holds)))
        def _():
            remote(rbuf, rall.at[k], sr.at[k], rr_sem.at[k], k, b).wait_send()

        return c

    lax.fori_loop(0, N_RES, wait_sent, 0)


def outer(back, msa, pair, wmix, wfac, tmat, amino, live):
    dma = pltpu.SemaphoreType.DMA
    vm = pl.BlockSpec(memory_space=pltpu.VMEM)
    jc = J_CHUNK * I_LOC
    return pl.pallas_call(
        outer_kernel,
        out_shape=(
            jax.ShapeDtypeStruct((S_LOC, I_LOC, CM), F32),
            jax.ShapeDtypeStruct((I_LOC, J_LOC, CZ), F32),
        ),
        in_specs=[vm] * 7 + [pl.BlockSpec(memory_space=pltpu.SMEM)],
        out_specs=(vm, vm),
        scratch_shapes=[
            pltpu.VMEM((1024, 1024), BF16),
            pltpu.VMEM((S_LOC * I_LOC, 128), F32),
            pltpu.VMEM((I_LOC * OPM, 128), F32),
            pltpu.VMEM((S_LOC, I_LOC * OPM), BF16),
            pltpu.VMEM((I_LOC, OPM * S_LOC), BF16),
            pltpu.VMEM((N_SEQ, S_LOC, I_LOC * OPM), BF16),
            pltpu.VMEM((N_RES, I_LOC, OPM * S_LOC), BF16),
            pltpu.VMEM((I_LOC // 2, 512, 256), BF16),
            pltpu.VMEM((1024, 256), BF16),
            pltpu.VMEM((8 * jc, 512), BF16),
            pltpu.VMEM((I_LOC, jc, 1024), BF16),
            dma((4,)), dma((4,)), dma((N_RES,)), dma((N_RES,)), dma((2,)),
        ],
        compiler_params=pltpu.CompilerParams(
            collective_id=1, has_side_effects=True, vmem_limit_bytes=VMEM_LIMIT
        ),
        name="outer",
    )(back, msa, pair, wmix, wfac, tmat, amino[:, None], live)


def on_device(msa, pair, amino, poly, live, w, wshift, shifts, wmix, wfac, tmat):
    qkvg, bias = project(msa, w, pair, wshift)
    qkvg = qkvg.reshape(N_RES, ROWS_PER, I_LOC, 128)
    bias = jnp.transpose(bias, (1, 0, 2)).astype(BF16)
    low = jnp.pad(bias, ((0, 0), (0, 0), (0, 64)))
    high = jnp.pad(bias, ((0, 0), (0, 0), (64, 0)))
    bias = jnp.where(lax.axis_index("seq") % 2 == 0, low, high)
    back = attend(qkvg, bias, poly, amino, shifts)
    return outer(back, msa, pair, wmix, wfac, tmat, amino, live)


def solution(mesh):
    in_specs = (P("seq", "res", None), P("res", "seq", None)) + (P(),) * 9
    out_specs = (P("seq", "res", None), P("res", "seq", None))
    return jax.shard_map(
        on_device, mesh=mesh, in_specs=in_specs, out_specs=out_specs, check_vma=False
    )
```

time: 924 us -> 140 us (0.15)
  waiting for transfers between devices: 501 us -> 0 us
  matrix products: 190 us -> 0 us
  Pallas kernels: 0 us -> 123 us
  local copies, waits for them, and re-layouts: 137 us -> 15 us
  blocking collectives: 63.8 us -> 0 us
  between operations: 14.3 us -> 0.66 us
  other arithmetic: 12.7 us -> 0.73 us
    all_gather x3 -> x0, waiting for transfers between devices: 415 us -> none  [the longest x1 160 us: on_device(): lax.all_gather(factors[:, :, opm_dim:], 'res', axis=1, tiled=True)]
    dot_general x7 -> x0, matrix products: 176 us -> none  [the longest x1 124 us: on_device(): jnp.einsum('jik,kz->jiz', outer, tensor_mean_matrix, precision=lax.Precis...]
    pallas_call x0 -> x3, Pallas kernels: none -> 123 us  [the longest x1 68.6 us: attend(): pl.pallas_call(attend_kernel, out_shape=jax.ShapeDtypeStruct((N_RES, 2, I...]
    reduce_scatter x1 -> x0, waiting for transfers between devices: 84.7 us -> none  [on_device(): lax.psum_scatter(jnp.einsum('jik,kz->jiz', outer, tensor_mean_matrix, pre...]
    transpose x2 -> x0, local copies, waits for them, and re-layouts: 79.4 us -> none  [the longest x1 75.2 us: on_device(): jnp.einsum('sic,sje->jice', left, right_all, preferred_element_type=jnp.f...]
    all_gather x1 -> x0, blocking collectives: 63.8 us -> none  [on_device(): bias = lax.all_gather(local_bias, 'seq', axis=2, tiled=True)]
    all_gather x4 -> x0, local copies, waits for them, and re-layouts: 49.6 us -> none  [the longest x1 16.7 us: on_device(): lax.all_gather(projected[:, :, feature_width:2 * feature_width], 'res', a...]
    sub x1 -> x0, matrix products: 13.6 us -> none  [on_device(): expo = jnp.exp(scores - row_max)]
  transfers between devices with their start and end apart: 4 -> 0, of which waited for: 4 -> 0; matrix products, arithmetic and copies ran while one was open for 5% -> 0% of each run, Pallas kernels for 0% -> 0%
where the time goes in v1:
time: 140 us
  Pallas kernels  123 us (88%)
  local copies, waits for them, and re-layouts  15 us (11%)
    pallas_call x1, Pallas kernels, attend(): pl.pallas_call(attend_kernel, out_shape=jax.ShapeDtypeStruct((N_RES, 2, I...  68.6 us
    pallas_call x1, Pallas kernels, outer(): pl.pallas_call(outer_kernel, out_shape=(jax.ShapeDtypeStruct((S_LOC, I_LO...  48.2 us
    unnamed x4, local copies, waits for them, and re-layouts  8.24 us
    pallas_call x1, Pallas kernels, project(): pl.pallas_call(project_kernel, out_shape=(jax.ShapeDtypeStruct((HEADS, GR...  6.44 us

profile of v1, /device:TPU:0, one launch (start us, length us, event | category | flops | bytes accessed | tf_op | source)
XLA Modules:
  0.0 139.7 jit_solution(18198592229802518705)
XLA Ops:
  0.6 1.3 broadcast_in_dim.16.amino_row
  1.9 1.3 broadcast_in_dim.14.poly_row
  3.2 1.4 %copy.16.wshift = f32[128,8]{1,0:T(8,128)} copy(f32[128,8]{0,1:T(8,128)} %param.17) | data formatting | bytes 8192 | tf_op args[6]
  4.6 1.5 %copy.20.wfac = bf16[256,64]{1,0:T(8,128)(2,1)} copy(bf16[256,64]{0,1:T(8,128)(2,1)} %param.20) | data formatting | bytes 65536 | tf_op args[9]
  6.1 1.6 %broadcast_in_dim.18.amino_col = s32[768,1]{1,0:T(8,128)} reshape(s32[768]{0:T(1024)} %param.13) | data formatting | bytes 6144 | tf_op jit(solution)/shard_map/broadcast_in_dim | solution.py:290
  7.7 1.6 %broadcast_in_dim.17.poly_col = s32[768,1]{1,0:T(8,128)} reshape(s32[768]{0:T(1024)} %param.14) | data formatting | bytes 6144 | tf_op jit(solution)/shard_map/broadcast_in_dim | solution.py:290
  9.3 6.4 %project.1 = (bf16[8,4,8,24,128]{4,3,2,1,0:T(8,128)(2,1)}, f32[24,8,192]{2,1,0:T(8,128)}) custom-call(f32[32,24,256]{2,1,0:T(8,128)} %msa.3, bf16[256,1024]{1,0:T(8,128)(2,1)} %w.1, f32[24,192,128]{2,1,0:T(8,128)} %pair.3, f32[128,8]{1,0:T(8,128)} %copy.16.wshift), custom_call_target="tpu_custom_call" | custom-call | tf_op jit(solution)/shard_map/project/pallas_call | solution.py:70
  15.7 1.0 copy.25
  16.7 0.7 pad_select_fusion.bias_in
  17.4 68.6 %attend.1.back = bf16[32,2,24,128]{3,2,1,0:T(8,128)(2,1)} custom-call(bf16[32,8,24,128]{3,2,1,0:T(8,128)(2,1)} %bitcast.4, bf16[8,24,256]{2,1,0:T(8,128)(2,1)} %pad_select_fusion.bias_in, s32[768,1]{1,0:T(8,128)} %broadcast_in_dim.17.poly_col, s32[1,768]{1,0:T(1,128)} %broadcast_in_dim.14.poly_row, s32[768,1]{1,0:T(8,128)} %broadcast_in_dim.18.amino_col, ...), custom_call_target="tpu_custom_call" | custom-call | tf_op jit(solution)/shard_map/attend/pallas_call | solution.py:271
  86.1 48.2 %outer.1 = (f32[32,24,256]{2,1,0:T(8,128)}, f32[24,192,128]{2,1,0:T(8,128)}) custom-call(bf16[32,2,24,128]{3,2,1,0:T(8,128)(2,1)} %attend.1.back, f32[32,24,256]{2,1,0:T(8,128)} %msa.3, f32[24,192,128]{2,1,0:T(8,128)} %pair.3, bf16[256,256]{1,0:T(8,128)(2,1)} %wmix.1, bf16[256,64]{1,0:T(8,128)(2,1)} %copy.20.wfac, f32[1024,128]{1,0:T(8,128)} %tmat.1, ...), custom_call_target="tpu_custom_call" | custom-call | tf_op jit(solution)/shard_map/outer/pallas_call | solution.py:498
  134.3 2.1 %copy.28 = f32[32,24,256]{2,1,0:T(8,128)} copy(f32[32,24,256]{2,1,0:T(8,128)} %get-tuple-element.8) | data formatting | bytes 1572864
  136.4 3.3 %copy.29 = f32[24,192,128]{2,1,0:T(8,128)} copy(f32[24,192,128]{2,1,0:T(8,128)} %get-tuple-element.9) | data formatting | bytes 4718592

commit v2 on v1

v2 whole, which is shorter than its diff:
```python
import math

import jax
import jax.numpy as jnp
from jax import lax
from jax.experimental import pallas as pl
from jax.experimental.pallas import tpu as pltpu
from jax.sharding import PartitionSpec as P

MESH = pl.DeviceIdType.MESH
F32 = jnp.float32
BF16 = jnp.bfloat16
LOG2E = math.log2(math.e)
VMEM_LIMIT = 58 * 1024 * 1024

N_RES, N_SEQ = 32, 4
S_LOC, I_LOC, J_LOC = 32, 24, 192
CM, CZ, HEADS, HD, OPM = 256, 128, 8, 32, 32
RES = 768
Q_CHUNK = 256
J_BLOCKS = 2
JC = J_BLOCKS * I_LOC


def lane_iota(shape):
    return lax.broadcasted_iota(jnp.int32, shape, len(shape) - 1)


def in_slot(lane, k):
    return (lane >= k * 32) & (lane < (k + 1) * 32)


def layer_norm(x):
    centre = jnp.mean(x, axis=-1, keepdims=True)
    d = x - centre
    spread = jnp.mean(d * d, axis=-1, keepdims=True)
    return d * lax.rsqrt(spread + 1e-05)


def nt_dot(a, b, precision=None):
    return lax.dot_general(
        a, b, (((1,), (1,)), ((), ())), precision=precision, preferred_element_type=F32
    )


def offset(k, r):
    kk = lax.rem(k * 11, N_RES)
    x = lax.rem(lax.div(r, 8) + lax.div(kk, 8), 4)
    y = lax.rem(lax.div(r, 4) + lax.div(kk, 4), 2)
    z = lax.rem(r + kk, 4)
    return x * 8 + y * 4 + z


def remote(src, dst, a, b, d, q):
    return pltpu.make_async_remote_copy(
        src_ref=src, dst_ref=dst, send_sem=a, recv_sem=b, device_id=(d, q), device_id_type=MESH
    )


def kernel(
    msa, pair, amino, poly, w, wshift_t, wmix, wfac_t, tmat, live, shifts,
    family, contact,
    btmp, bsend, b1, br, bias, pgate, gate, qsend, recv, qs, ks, vs, acc, ret, back,
    bd_mix, fac, tr, lbuf, rbuf, lall, rall, bd, tcat, lhs, amat,
    ss, rs, s1, r1, s2, r2, s3, r3, sb, rb, sl, rl, sr, rr_sem, loc, locb,
):
    r, s = lax.axis_index("res"), lax.axis_index("seq")
    h, z = lax.div(r, 4), lax.rem(r, 4)
    y_lo = lax.rem(h, 2)
    s_y = lax.rem(s + 2, 4)
    s_c = s + 1 - 2 * lax.rem(s, 2)
    b, mine = lax.div(r, 8), lax.rem(r, 8) * 4 + s
    holds = b == s

    def source(k):
        return 8 * s + lax.div(k, 4), lax.rem(k, 4)

    barrier = pltpu.get_barrier_semaphore()

    def greet(k, c):
        pl.semaphore_signal(barrier, inc=1, device_id=(offset(k, r), s), device_id_type=MESH)
        return c

    lax.fori_loop(1, N_RES, greet, 0)

    def greet_y(k, c):
        pl.semaphore_signal(barrier, inc=1, device_id=(h * 4 + k, s_y), device_id_type=MESH)
        return c

    lax.fori_loop(0, 4, greet_y, 0)

    def greet_seq(k, c):
        pl.semaphore_signal(barrier, inc=1, device_id=(r, lax.rem(s + k, 4)), device_id_type=MESH)
        return c

    lax.fori_loop(1, N_SEQ, greet_seq, 0)

    def greet_right(k, c):
        rr, q = source(k)

        @pl.when(jnp.logical_or(rr != r, q != s))
        def _():
            pl.semaphore_signal(barrier, inc=1, device_id=(rr, q), device_id_type=MESH)

        return c

    lax.fori_loop(0, N_RES, greet_right, 0)

    btmp[...] = jnp.zeros_like(btmp)
    chunk = 4
    for i0 in range(0, I_LOC, chunk):
        zn = layer_norm(pair[i0 : i0 + chunk].reshape(chunk * J_LOC, CZ))
        bb = nt_dot(wshift_t[...], zn, lax.Precision.HIGHEST)
        for i in range(chunk):
            rows, col = slice((i0 + i) * HEADS, (i0 + i + 1) * HEADS), i * J_LOC
            btmp[0, rows, :] = bb[:, col : col + 128]
            btmp[1, rows, 0:64] = bb[:, col + 128 : col + J_LOC]
    odd = jnp.full((I_LOC, 256), lax.rem(s, 2), jnp.int32) > 0
    for hh in range(HEADS):
        v = jnp.concatenate(
            [btmp[n, pl.ds(hh, I_LOC, stride=HEADS), :] for n in range(2)], axis=1
        )
        bsend[hh] = jnp.where(odd, pltpu.roll(v, 64, 1), v).astype(BF16)

    pl.semaphore_wait(barrier, 31 + 4 + 3 + N_RES - holds.astype(jnp.int32))

    own1 = pltpu.make_async_copy(bsend.at[h], b1.at[h], loc.at[1])
    own1.start()

    def send1(k, c):
        hh = lax.rem(h + k, 8)
        remote(bsend.at[hh], b1.at[h], s1.at[hh], r1.at[h], hh * 4 + z, s).start()
        return c

    lax.fori_loop(1, 8, send1, 0)

    normed = layer_norm(msa[...].reshape(S_LOC * I_LOC, CM)).astype(BF16)
    lane3 = lane_iota((8, I_LOC, 128))
    for part in range(3):
        out = jnp.dot(normed, w[:, part * CM : (part + 1) * CM], preferred_element_type=F32)
        if part == 0:
            out = out * F32(LOG2E / math.sqrt(HD))
        for t in range(2):
            cols = out[:, t * 128 : (t + 1) * 128].reshape(8, 4, I_LOC, 128)
            for a in range(4):
                tile = None
                for k in range(4):
                    piece = cols[:, k]
                    if (k - a) % 4:
                        piece = pltpu.roll(piece, (k - a) % 4 * 32, 2)
                    tile = piece if tile is None else jnp.where(in_slot(lane3, k), piece, tile)
                tile = tile.astype(BF16)
                for g in range(4):
                    for half in range(2):
                        qsend[(t * 4 + a) * 4 + g, half, part] = tile[g * 2 + half]

    def wait1(k, c):
        hh = lax.rem(h + k, 8)
        remote(bsend.at[hh], b1.at[hh], s1.at[hh], r1.at[hh], hh * 4 + z, s).wait_recv()
        return c

    lax.fori_loop(1, 8, wait1, 0)
    own1.wait()
    own2 = pltpu.make_async_copy(b1, br.at[s, z], loc.at[2])
    own2.start()

    def send2(k, c):
        zz = lax.rem(z + k, 4)
        q = lax.rem(s + 2 * lax.div(k, 4), 4)
        remote(b1, br.at[s, z], s2.at[k], r2.at[lax.div(s, 2) * 4 + z], h * 4 + zz, q).start()
        return c

    lax.fori_loop(1, 8, send2, 0)

    for half in range(2):
        pltpu.make_async_copy(qsend.at[r, half], recv.at[half, r], locb.at[half]).start()

        def send(k, c, half=half):
            d = offset(k, r)
            remote(qsend.at[d, half], recv.at[half, r], ss.at[half, d], rs.at[half, r], d, s).start()
            return c

        lax.fori_loop(1, N_RES, send, 0)

    pgate[...] = jnp.dot(normed, w[:, 3 * CM :], preferred_element_type=F32).astype(BF16).astype(F32)
    for t in range(2):
        cols = jax.nn.sigmoid(pgate[:, t * 128 : (t + 1) * 128]).reshape(8, 4, I_LOC, 128)
        for a in range(4):
            tile = None
            for k in range(4):
                piece = cols[:, k]
                if (k - a) % 4:
                    piece = pltpu.roll(piece, (k - a) % 4 * 32, 2)
                tile = piece if tile is None else jnp.where(in_slot(lane3, k), piece, tile)
            for g in range(4):
                for half in range(2):
                    gate[half, t * 4 + a, g] = tile[g * 2 + half]
    bd_mix[...] = jnp.zeros_like(bd_mix)
    for hh in range(HEADS):
        for k in range(4):
            bd_mix[hh * 128 + k * 32 : hh * 128 + (k + 1) * 32, k * CM : (k + 1) * CM] = wmix[
                hh * HD : (hh + 1) * HD, :
            ]
    for e in range(OPM):
        t = tmat[pl.ds(e, OPM, stride=OPM), :]
        head = t.astype(BF16)
        tcat[e * 32 : (e + 1) * 32, 0:128] = head
        tcat[e * 32 : (e + 1) * 32, 128:256] = (t - head.astype(F32)).astype(BF16)
    acc[...] = jnp.zeros_like(acc)
    amino_row = amino[...].reshape(1, RES)
    poly_row = poly[...].reshape(1, RES)

    def column(row, n):
        tile = row[:, n * 128 : (n + 1) * 128].astype(F32)
        return jnp.transpose(jnp.broadcast_to(tile, (128, 128)), (1, 0))

    amino_col = [column(amino_row, n) for n in range(6)]
    for n in range(6):
        fac[n * 128 : (n + 1) * 128, :] = column(poly_row, n)

    def wait2(k, c):
        zz = lax.rem(z + k, 4)
        q = lax.rem(s + 2 * lax.div(k, 4), 4)
        remote(b1, br.at[q, zz], s2.at[k], r2.at[lax.div(q, 2) * 4 + zz], h * 4 + zz, q).wait_recv()
        return c

    lax.fori_loop(1, 8, wait2, 0)
    own2.wait()
    for t in range(2):
        q = lax.rem(s + 2 * t, 4)
        remote(br.at[q], br.at[q], s3.at[lax.div(q, 2)], r3.at[lax.div(q, 2)], r, s_c).start()
    for t in range(2):
        q = lax.rem(s + 2 * t, 4)
        qc = q + 1 - 2 * lax.rem(q, 2)
        remote(br.at[qc], br.at[qc], s3.at[lax.div(q, 2)], r3.at[lax.div(q, 2)], r, s_c).wait_recv()

    shift = shifts[h]
    lane24 = lane_iota((I_LOC, 128))
    poly_f = poly_row.astype(F32)

    def build(k, c):
        zz, hh = lax.rem(k, 4), lax.div(k, 4)
        row = pl.multiple_of(k * I_LOC, 8)
        own = fac[pl.ds(row, I_LOC), :]
        t = [br[q, zz, hh].astype(F32) for q in range(4)]
        tiles = [
            t[0][:, :128],
            jnp.where(lane24 < 64, t[0][:, 128:], t[1][:, :128]),
            t[1][:, 128:],
            t[2][:, :128],
            jnp.where(lane24 < 64, t[2][:, 128:], t[3][:, :128]),
            t[3][:, 128:],
        ]
        for n in range(6):
            cols = slice(n * 128, (n + 1) * 128)
            full = tiles[n] + jnp.where(own != poly_f[:, cols], shift, F32(0.0))
            full = jnp.where(amino_row[:, cols] > 0, full * F32(LOG2E), F32(-1e9))
            bias[pl.ds(row, I_LOC), cols] = full
        return c

    lax.fori_loop(0, N_RES, build, 0)

    lane_q = lane_iota((Q_CHUNK, 128))
    lane = lane_iota((RES, 128))
    for half in range(2):

        def wait_in(k, c, half=half):
            d = offset(k, r)
            remote(
                qsend.at[d, half], recv.at[half, d], ss.at[half, d], rs.at[half, d], d, s
            ).wait_recv()
            return c

        lax.fori_loop(1, N_RES, wait_in, 0)
        pltpu.make_async_copy(qsend.at[r, half], recv.at[half, r], locb.at[half]).wait()
        qs[...] = recv[half, :, 0].astype(F32).reshape(RES, 128).astype(BF16)
        kf = recv[half, :, 1].astype(F32).reshape(RES, 128)
        for n in range(6):
            rows = slice(n * 128, (n + 1) * 128)
            ks[rows, :] = jnp.where(amino_col[n] > 0, kf[rows], F32(0.0)).astype(BF16)
        vs[...] = recv[half, :, 2].astype(F32).reshape(RES, 128).astype(BF16)

        def one_row(rr, c, half=half):
            slot = in_slot(lane, rr)
            xv = jnp.where(slot, vs[...].astype(F32), F32(1.0)).astype(BF16)
            xk = ks[...]
            slot_q = in_slot(lane_q, rr)
            for q0 in range(0, RES, Q_CHUNK):
                rows = slice(q0, q0 + Q_CHUNK)
                xq = jnp.where(slot_q, qs[rows, :].astype(F32), F32(0.0)).astype(BF16)
                sc = nt_dot(xq, xk) + bias[rows, :]
                m = jnp.max(sc, axis=-1, keepdims=True)
                p = jnp.exp2(sc - m).astype(BF16)
                o = jnp.dot(p, xv, preferred_element_type=F32)
                o = o / pltpu.roll(o, 32, 1)
                acc[half, rows, :] = jnp.where(slot_q, o, acc[half, rows, :])
            return c

        lax.fori_loop(0, 4, one_row, 0)
        ret[half] = acc[half].reshape(N_RES, I_LOC, 128).astype(BF16)
        pltpu.make_async_copy(ret.at[half, r], back.at[half, r], locb.at[2 + half]).start()

        def send_back(k, c, half=half):
            d = offset(k, r)
            remote(ret.at[half, d], back.at[half, r], sb.at[half, d], rb.at[half, r], d, s).start()
            return c

        lax.fori_loop(1, N_RES, send_back, 0)

    for n in range(6):
        tr[n * 128 : (n + 1) * 128, :] = amino_col[n]
    own_live = tr[pl.ds(pl.multiple_of(r * I_LOC, 8), I_LOC), :]
    for half in range(2):

        def wait_back(k, c, half=half):
            d = offset(k, r)
            remote(
                ret.at[half, d], back.at[half, d], sb.at[half, d], rb.at[half, d], d, s
            ).wait_recv()
            return c

        lax.fori_loop(1, N_RES, wait_back, 0)
        pltpu.make_async_copy(ret.at[half, r], back.at[half, r], locb.at[2 + half]).wait()
        gated = jnp.concatenate(
            [
                (back[half, 4 * hh : 4 * hh + 4].astype(F32) * gate[half, hh]).reshape(4 * I_LOC, 128)
                for hh in range(HEADS)
            ],
            axis=1,
        ).astype(BF16)
        for k in range(4):
            delta = jnp.dot(
                gated, bd_mix[:, k * CM : (k + 1) * CM], preferred_element_type=F32
            ).reshape(4, I_LOC, CM)
            fams = []
            for g in range(4):
                row = g * 8 + half * 4 + k
                fam = msa[row] + live[s * S_LOC + row].astype(F32) * delta[g]
                family[row] = fam
                fams.append(fam)
            y = layer_norm(jnp.concatenate(fams, axis=0)).astype(BF16)
            f = nt_dot(y, wfac_t[...])
            f = jnp.concatenate([f, jnp.zeros((4 * I_LOC, 64), F32)], axis=1)
            for g in range(4):
                row = g * 8 + half * 4 + k
                on = live[s * S_LOC + row].astype(F32)
                fac[row * I_LOC : (row + 1) * I_LOC, :] = f[g * I_LOC : (g + 1) * I_LOC] * (
                    on * own_live
                )

    lane32 = lane_iota((S_LOC, 128))
    for i0 in range(0, I_LOC, 4):
        tile = None
        for k in range(4):
            i = i0 + k
            f = fac[pl.ds(i, S_LOC, stride=I_LOC), :]
            moved = pltpu.roll(f, k * 32, 1) if k else f
            tile = moved if tile is None else jnp.where(in_slot(lane32, k), moved, tile)
            ft = jnp.transpose(f, (1, 0))[OPM : 2 * OPM, :]
            tr[i * OPM : (i + 1) * OPM, :] = jnp.concatenate(
                [ft, jnp.zeros((OPM, 128 - S_LOC), F32)], axis=1
            )
        lbuf[:, i0 * 32 : (i0 + 4) * 32] = tile.astype(BF16)
    for e0 in range(0, OPM, 4):
        tile = tr[pl.ds(e0, I_LOC, stride=OPM), :]
        for k in range(1, 4):
            moved = pltpu.roll(tr[pl.ds(e0 + k, I_LOC, stride=OPM), :], k * 32, 1)
            tile = jnp.where(in_slot(lane24, k), moved, tile)
        rbuf[:, e0 * 32 : (e0 + 4) * 32] = tile.astype(BF16)

    def send_left(k, c):
        q = lax.rem(s + k, 4)
        remote(lbuf, lall.at[s], sl.at[q], rl.at[s], r, q).start()
        return c

    lax.fori_loop(1, N_SEQ, send_left, 0)

    def yz(k):
        kk = lax.rem(k * 3, 8)
        return lax.div(kk, 4), lax.rem(kk, 4)

    def target(k):
        dy, dz = yz(lax.div(k, 4))
        x = lax.rem(b + k, 4)
        return x * 8 + lax.rem(y_lo + dy, 2) * 4 + lax.rem(z + dz, 4)

    def send_right(k, c):
        d = target(k)

        @pl.when(jnp.logical_or(k != 0, jnp.logical_not(holds)))
        def _():
            remote(rbuf, rall.at[mine], sr.at[d], rr_sem.at[mine], d, b).start()

        return c

    lax.fori_loop(0, N_RES, send_right, 0)
    ownl = pltpu.make_async_copy(lbuf, lall.at[s], loc.at[0])
    ownl.start()

    @pl.when(holds)
    def _():
        cp = pltpu.make_async_copy(rbuf, rall.at[mine], loc.at[3])
        cp.start()
        cp.wait()

    def wait_left(k, c):
        q = lax.rem(s + k, 4)
        remote(lbuf, lall.at[q], sl.at[q], rl.at[q], r, q).wait_recv()
        return c

    lax.fori_loop(1, N_SEQ, wait_left, 0)
    ownl.wait()
    sel_r = lax.broadcasted_iota(jnp.int32, (128, 512), 0)
    sel_c = lax.broadcasted_iota(jnp.int32, (128, 512), 1)
    same = (lax.div(sel_r, 32) == lax.div(sel_c, 128)) & (lax.rem(sel_r, 32) == lax.rem(sel_c, 32))
    sel = jnp.where(same, F32(1.0), F32(0.0)).astype(BF16)
    for i0 in range(0, I_LOC, 4):
        for q in range(N_SEQ):
            rep = jnp.dot(lall[q, :, i0 * 32 : (i0 + 4) * 32], sel, preferred_element_type=F32)
            for k in range(4):
                i = i0 + k
                piece = rep[:, k * 128 : (k + 1) * 128]
                for e in range(4):
                    bd[
                        i // 2,
                        q * 128 + e * 32 : q * 128 + (e + 1) * 32,
                        (i % 2) * 128 : (i % 2 + 1) * 128,
                    ] = jnp.where(in_slot(lane32, e), piece, F32(0.0)).astype(BF16)

    count = lax.fori_loop(0, 128, lambda k, c: c + live[k], jnp.int32(0)).astype(F32)
    inv = 1.0 / jnp.maximum(jnp.full((1, 128), count, F32), 1.0)

    for c0 in range(0, 8, J_BLOCKS):
        blocks = []
        for t in range(J_BLOCKS):
            dy, dz = yz(c0 + t)
            blocks.append(lax.rem(y_lo + 2 - dy, 2) * 4 + lax.rem(z + 4 - dz, 4))
        for blk in blocks:

            def wait_right(q, c, blk=blk):
                rr = 8 * s + blk

                @pl.when(jnp.logical_or(rr != r, q != s))
                def _():
                    k = blk * 4 + q
                    remote(rbuf, rall.at[k], sr.at[k], rr_sem.at[k], rr, q).wait_recv()

                return c

            lax.fori_loop(0, N_SEQ, wait_right, 0)
        for q in range(N_SEQ):
            for g in range(8):
                cols = slice(g * 128, (g + 1) * 128)
                rows = jnp.concatenate(
                    [rall[blk * 4 + q, :, cols].astype(F32) for blk in blocks], axis=0
                )
                lhs[g * JC : (g + 1) * JC, q * 128 : (q + 1) * 128] = rows.astype(BF16)

        def pair_of(p, c):
            a = jnp.dot(lhs[...], bd[p], preferred_element_type=F32).astype(BF16)
            for half in range(2):
                for g in range(8):
                    amat[2 * p + half, :, g * 128 : (g + 1) * 128] = a[
                        g * JC : (g + 1) * JC, half * 128 : (half + 1) * 128
                    ]
            return c

        lax.fori_loop(0, I_LOC // 2, pair_of, 0)

        def finish(p, c, blocks=tuple(blocks)):
            am = amat[pl.ds(12 * p, 12)].reshape(12 * JC, 1024)
            o = jnp.dot(am, tcat[...], preferred_element_type=F32)
            o = ((o[:, :128] + o[:, 128:]) * inv).reshape(12, JC, CZ)
            for t, blk in enumerate(blocks):
                at = (pl.ds(12 * p, 12), pl.ds(pl.multiple_of(blk * I_LOC, 8), I_LOC))
                contact[at] = pair[at] + o[:, t * I_LOC : (t + 1) * I_LOC]
            return c

        lax.fori_loop(0, I_LOC // 12, finish, 0)

    def sent1(k, c):
        hh = lax.rem(h + k, 8)
        remote(bsend.at[hh], b1.at[hh], s1.at[hh], r1.at[hh], hh * 4 + z, s).wait_send()
        remote(b1, br.at[s, z], s2.at[k], r2.at[k], r, s_c).wait_send()
        return c

    lax.fori_loop(1, 8, sent1, 0)
    for t in range(2):
        q = lax.rem(s + 2 * t, 4)
        remote(br.at[q], br.at[q], s3.at[lax.div(q, 2)], r3.at[lax.div(q, 2)], r, s_c).wait_send()

    def sent(k, c):
        d = offset(k, r)
        for half in range(2):
            remote(
                qsend.at[d, half], recv.at[half, d], ss.at[half, d], rs.at[half, d], d, s
            ).wait_send()
            remote(
                ret.at[half, d], back.at[half, d], sb.at[half, d], rb.at[half, d], d, s
            ).wait_send()
        return c

    lax.fori_loop(1, N_RES, sent, 0)

    def sent_left(k, c):
        q = lax.rem(s + k, 4)
        remote(lbuf, lall.at[q], sl.at[q], rl.at[q], r, q).wait_send()
        return c

    lax.fori_loop(1, N_SEQ, sent_left, 0)

    def sent_right(k, c):
        @pl.when(jnp.logical_or(k != r, jnp.logical_not(holds)))
        def _():
            remote(rbuf, rall.at[k], sr.at[k], rr_sem.at[k], k, b).wait_send()

        return c

    lax.fori_loop(0, N_RES, sent_right, 0)


def on_device(msa, pair, amino, poly, live, w, wshift, shifts, wmix, wfac, tmat):
    dma = pltpu.SemaphoreType.DMA
    vm = pl.BlockSpec(memory_space=pltpu.VMEM)
    sm = pl.BlockSpec(memory_space=pltpu.SMEM)
    return pl.pallas_call(
        kernel,
        out_shape=(
            jax.ShapeDtypeStruct((S_LOC, I_LOC, CM), F32),
            jax.ShapeDtypeStruct((I_LOC, J_LOC, CZ), F32),
        ),
        in_specs=[vm] * 9 + [sm] * 2,
        out_specs=(vm, vm),
        scratch_shapes=[
            pltpu.VMEM((2, I_LOC * HEADS, 128), F32),
            pltpu.VMEM((HEADS, I_LOC, 256), BF16),
            pltpu.VMEM((HEADS, I_LOC, 256), BF16),
            pltpu.VMEM((N_SEQ, 4, HEADS, I_LOC, 256), BF16),
            pltpu.VMEM((RES, RES), F32),
            pltpu.VMEM((RES, CM), F32),
            pltpu.VMEM((2, HEADS, 4, I_LOC, 128), F32),
            pltpu.VMEM((N_RES, 2, 3, I_LOC, 128), BF16),
            pltpu.VMEM((2, N_RES, 3, I_LOC, 128), BF16),
            pltpu.VMEM((RES, 128), BF16),
            pltpu.VMEM((RES, 128), BF16),
            pltpu.VMEM((RES, 128), BF16),
            pltpu.VMEM((2, RES, 128), F32),
            pltpu.VMEM((2, N_RES, I_LOC, 128), BF16),
            pltpu.VMEM((2, N_RES, I_LOC, 128), BF16),
            pltpu.VMEM((1024, 1024), BF16),
            pltpu.VMEM((S_LOC * I_LOC, 128), F32),
            pltpu.VMEM((I_LOC * OPM, 128), F32),
            pltpu.VMEM((S_LOC, I_LOC * OPM), BF16),
            pltpu.VMEM((I_LOC, OPM * S_LOC), BF16),
            pltpu.VMEM((N_SEQ, S_LOC, I_LOC * OPM), BF16),
            pltpu.VMEM((N_RES, I_LOC, OPM * S_LOC), BF16),
            pltpu.VMEM((I_LOC // 2, 512, 256), BF16),
            pltpu.VMEM((1024, 256), BF16),
            pltpu.VMEM((8 * JC, 512), BF16),
            pltpu.VMEM((I_LOC, JC, 1024), BF16),
            dma((2, N_RES)), dma((2, N_RES)),
            dma((8,)), dma((8,)), dma((8,)), dma((8,)), dma((2,)), dma((2,)),
            dma((2, N_RES)), dma((2, N_RES)),
            dma((4,)), dma((4,)), dma((N_RES,)), dma((N_RES,)),
            dma((4,)), dma((4,)),
        ],
        compiler_params=pltpu.CompilerParams(
            collective_id=0, has_side_effects=True, vmem_limit_bytes=VMEM_LIMIT
        ),
        name="evoformer",
    )(msa, pair, amino, poly, w, wshift.T, wmix, wfac.T, tmat, live, shifts)


def solution(mesh):
    in_specs = (P("seq", "res", None), P("res", "seq", None)) + (P(),) * 9
    out_specs = (P("seq", "res", None), P("res", "seq", None))
    return jax.shard_map(
        on_device, mesh=mesh, in_specs=in_specs, out_specs=out_specs, check_vma=False
    )
```

time: 140 us -> 114 us (0.81)
  the two profiles are of different devices: /device:TPU:0 before, /device:TPU:5 now
where the time goes in v2:
time: 114 us
  Pallas kernels  108 us (95%)
  local copies, waits for them, and re-layouts  5.36 us (5%)
    pallas_call x1, Pallas kernels, on_device(): pl.pallas_call(kernel, out_shape=(jax.ShapeDtypeStruct((S_LOC, I_LOC, CM)...  108 us
    unnamed x2, local copies, waits for them, and re-layouts  5.36 us

profile of v2, /device:TPU:5, one launch (start us, length us, event | category | flops | bytes accessed | tf_op | source)
XLA Modules:
  0.0 114.1 jit_solution(17903921442227609113)
XLA Ops:
  0.6 108.1 %evoformer.1 = (f32[32,24,256]{2,1,0:T(8,128)}, f32[24,192,128]{2,1,0:T(8,128)}) custom-call(f32[32,24,256]{2,1,0:T(8,128)} %msa.1, f32[24,192,128]{2,1,0:T(8,128)} %pair.1, s32[768]{0:T(1024)} %amino.1, s32[768]{0:T(1024)} %poly.1, bf16[256,1024]{1,0:T(8,128)(2,1)} %w.1, f32[8,128]{1,0:T(8,128)} %bitcast.3, bf16[256,256]{1,0:T(8,128)(2,1)} %wmix.1, ...), custom_call_target="tpu_custom_call" | custom-call | tf_op jit(solution)/shard_map/evoformer/pallas_call | solution.py:526
  108.7 2.1 %copy.15 = f32[32,24,256]{2,1,0:T(8,128)} copy(f32[32,24,256]{2,1,0:T(8,128)} %get-tuple-element.4) | data formatting | bytes 1572864
  110.8 3.3 %copy.16 = f32[24,192,128]{2,1,0:T(8,128)} copy(f32[24,192,128]{2,1,0:T(8,128)} %get-tuple-element.5) | data formatting | bytes 4718592

commit v3 on v2

v3 whole, which is shorter than its diff:
```python
import math

import jax
import jax.numpy as jnp
from jax import lax
from jax.experimental import pallas as pl
from jax.experimental.pallas import tpu as pltpu
from jax.sharding import PartitionSpec as P

MESH = pl.DeviceIdType.MESH
F32 = jnp.float32
BF16 = jnp.bfloat16
LOG2E = math.log2(math.e)
VMEM_LIMIT = 58 * 1024 * 1024

N_RES, N_SEQ = 32, 4
S_LOC, I_LOC, J_LOC = 32, 24, 192
CM, CZ, HEADS, HD, OPM = 256, 128, 8, 32, 32
RES = 768
Q_CHUNK = 256
J_BLOCKS = 2
JC = J_BLOCKS * I_LOC


def lane_iota(shape):
    return lax.broadcasted_iota(jnp.int32, shape, len(shape) - 1)


def in_slot(lane, k):
    return (lane >= k * 32) & (lane < (k + 1) * 32)


def layer_norm(x):
    centre = jnp.mean(x, axis=-1, keepdims=True)
    d = x - centre
    spread = jnp.mean(d * d, axis=-1, keepdims=True)
    return d * lax.rsqrt(spread + 1e-05)


def nt_dot(a, b, precision=None):
    return lax.dot_general(
        a, b, (((1,), (1,)), ((), ())), precision=precision, preferred_element_type=F32
    )


def offset(k, r):
    kk = lax.rem(k * 11, N_RES)
    x = lax.rem(lax.div(r, 8) + lax.div(kk, 8), 4)
    y = lax.rem(lax.div(r, 4) + lax.div(kk, 4), 2)
    z = lax.rem(r + kk, 4)
    return x * 8 + y * 4 + z


def exchange_lanes(tiles, width):
    lane = lane_iota(tiles[0].shape)
    tiles, bit = list(tiles), 1
    while bit < len(tiles):
        low = lax.rem(lane, 2 * bit * width) < bit * width
        new = list(tiles)
        for k in range(len(tiles)):
            if not k & bit:
                a, b = tiles[k], tiles[k | bit]
                new[k] = jnp.where(low, a, pltpu.roll(b, bit * width, 1))
                new[k | bit] = jnp.where(low, pltpu.roll(a, 128 - bit * width, 1), b)
        tiles, bit = new, 2 * bit
    return tiles


def remote(src, dst, a, b, d, q):
    return pltpu.make_async_remote_copy(
        src_ref=src, dst_ref=dst, send_sem=a, recv_sem=b, device_id=(d, q), device_id_type=MESH
    )


def kernel(
    msa, pair, amino, poly, w, wshift_t, wmix, wfac_t, tmat, live, shifts,
    family, contact,
    btmp, bsend, b1, br, bias, pgate, gate, qsend, recv, qs, ks, vs, acc, ret, back,
    bd_mix, fac, tr, lbuf, rbuf, lall, rall, lw, tcat, lhs, amat,
    ss, rs, s1, r1, s2, r2, s3, r3, sb, rb, sl, rl, sr, rr_sem, loc,
):
    r, s = lax.axis_index("res"), lax.axis_index("seq")
    h, z = lax.div(r, 4), lax.rem(r, 4)
    y_lo = lax.rem(h, 2)
    s_y = lax.rem(s + 2, 4)
    s_c = s + 1 - 2 * lax.rem(s, 2)
    b, mine = lax.div(r, 8), lax.rem(r, 8) * 4 + s
    holds = b == s

    def source(k):
        return 8 * s + lax.div(k, 4), lax.rem(k, 4)

    barrier = pltpu.get_barrier_semaphore()

    def greet(k, c):
        pl.semaphore_signal(barrier, inc=1, device_id=(offset(k, r), s), device_id_type=MESH)
        return c

    lax.fori_loop(1, N_RES, greet, 0)

    def greet_y(k, c):
        pl.semaphore_signal(barrier, inc=1, device_id=(h * 4 + k, s_y), device_id_type=MESH)
        return c

    lax.fori_loop(0, 4, greet_y, 0)

    def greet_seq(k, c):
        pl.semaphore_signal(barrier, inc=1, device_id=(r, lax.rem(s + k, 4)), device_id_type=MESH)
        return c

    lax.fori_loop(1, N_SEQ, greet_seq, 0)

    def greet_right(k, c):
        rr, q = source(k)

        @pl.when(jnp.logical_or(rr != r, q != s))
        def _():
            pl.semaphore_signal(barrier, inc=1, device_id=(rr, q), device_id_type=MESH)

        return c

    lax.fori_loop(0, N_RES, greet_right, 0)

    btmp[...] = jnp.zeros_like(btmp)
    chunk = 4
    for i0 in range(0, I_LOC, chunk):
        zn = layer_norm(pair[i0 : i0 + chunk].reshape(chunk * J_LOC, CZ))
        bb = nt_dot(wshift_t[...], zn, lax.Precision.HIGHEST)
        for i in range(chunk):
            rows, col = slice((i0 + i) * HEADS, (i0 + i + 1) * HEADS), i * J_LOC
            btmp[0, rows, :] = bb[:, col : col + 128]
            btmp[1, rows, 0:64] = bb[:, col + 128 : col + J_LOC]
    odd = jnp.full((I_LOC, 256), lax.rem(s, 2), jnp.int32) > 0
    for hh in range(HEADS):
        v = jnp.concatenate(
            [btmp[n, pl.ds(hh, I_LOC, stride=HEADS), :] for n in range(2)], axis=1
        )
        bsend[hh] = jnp.where(odd, pltpu.roll(v, 64, 1), v).astype(BF16)

    pl.semaphore_wait(barrier, 31 + 4 + 3 + N_RES - holds.astype(jnp.int32))

    pltpu.make_async_copy(bsend.at[h], b1.at[h], r1).start()

    def send1(k, c):
        hh = lax.rem(h + k, 8)
        remote(bsend.at[hh], b1.at[h], s1, r1, hh * 4 + z, s).start()
        return c

    lax.fori_loop(1, 8, send1, 0)

    normed = layer_norm(msa[...].reshape(S_LOC * I_LOC, CM)).astype(BF16)
    lane3 = lane_iota((8, I_LOC, 128))
    for part in range(3):
        out = jnp.dot(normed, w[:, part * CM : (part + 1) * CM], preferred_element_type=F32)
        if part == 0:
            out = out * F32(LOG2E / math.sqrt(HD))
        for t in range(2):
            cols = out[:, t * 128 : (t + 1) * 128].reshape(8, 4, I_LOC, 128)
            for a in range(4):
                tile = None
                for k in range(4):
                    piece = cols[:, k]
                    if (k - a) % 4:
                        piece = pltpu.roll(piece, (k - a) % 4 * 32, 2)
                    tile = piece if tile is None else jnp.where(in_slot(lane3, k), piece, tile)
                tile = tile.astype(BF16)
                for g in range(4):
                    for half in range(2):
                        qsend[(t * 4 + a) * 4 + g, half, part] = tile[g * 2 + half]

    def send_rows(half):
        pltpu.make_async_copy(qsend.at[r, half], recv.at[half, r], rs.at[half]).start()

        def send(k, c):
            d = offset(k, r)
            remote(qsend.at[d, half], recv.at[half, r], ss, rs.at[half], d, s).start()
            return c

        lax.fori_loop(1, N_RES, send, 0)

    send_rows(0)
    pltpu.make_async_copy(bsend, b1, r1).wait()
    slot = s * 4 + z
    own2 = pltpu.make_async_copy(b1, br.at[slot], loc.at[0])
    own2.start()

    def send2(k, c):
        zz = lax.rem(z + k, 4)
        q = lax.rem(s + 2 * lax.div(k, 4), 4)
        remote(b1, br.at[slot], s2, r2.at[lax.div(s, 2) * 4 + z], h * 4 + zz, q).start()
        return c

    lax.fori_loop(1, 8, send2, 0)
    remote(b1, br.at[slot], s3, r3, r, s_c).start()

    pgate[...] = jnp.dot(normed, w[:, 3 * CM :], preferred_element_type=F32).astype(BF16).astype(F32)
    for t in range(2):
        cols = jax.nn.sigmoid(pgate[:, t * 128 : (t + 1) * 128]).reshape(8, 4, I_LOC, 128)
        for a in range(4):
            tile = None
            for k in range(4):
                piece = cols[:, k]
                if (k - a) % 4:
                    piece = pltpu.roll(piece, (k - a) % 4 * 32, 2)
                tile = piece if tile is None else jnp.where(in_slot(lane3, k), piece, tile)
            for g in range(4):
                for half in range(2):
                    gate[half, t * 4 + a, g] = tile[g * 2 + half]
    bd_mix[...] = jnp.zeros_like(bd_mix)
    for hh in range(HEADS):
        for k in range(4):
            bd_mix[hh * 128 + k * 32 : hh * 128 + (k + 1) * 32, k * CM : (k + 1) * CM] = wmix[
                hh * HD : (hh + 1) * HD, :
            ]
    for e in range(OPM):
        t = tmat[pl.ds(e, OPM, stride=OPM), :]
        head = t.astype(BF16)
        tcat[e * 32 : (e + 1) * 32, 0:128] = head
        tcat[e * 32 : (e + 1) * 32, 128:256] = (t - head.astype(F32)).astype(BF16)
    acc[...] = jnp.zeros_like(acc)
    amino_row = amino[...].reshape(1, RES)
    poly_row = poly[...].reshape(1, RES)

    def column(row, n):
        tile = row[:, n * 128 : (n + 1) * 128].astype(F32)
        return jnp.transpose(jnp.broadcast_to(tile, (128, 128)), (1, 0))

    amino_col = [column(amino_row, n) for n in range(6)]
    for n in range(6):
        fac[n * 128 : (n + 1) * 128, :] = column(poly_row, n)

    remote(br.at[pl.ds(0, 7)], br.at[pl.ds(0, 7)], s2, r3, r, s_c).wait_send()
    send_rows(1)

    def wait2(k, c):
        zz = lax.rem(z + k, 4)
        q = lax.rem(s + 2 * lax.div(k, 4), 4)
        at = q * 4 + zz
        remote(b1, br.at[at], s2, r2.at[lax.div(q, 2) * 4 + zz], h * 4 + zz, q).wait_recv()
        remote(br.at[at], br.at[at], s3, r3, r, s_c).start()
        return c

    lax.fori_loop(1, 8, wait2, 0)
    own2.wait()
    remote(br.at[pl.ds(0, 8)], br.at[pl.ds(0, 8)], s3, r3, r, s_c).wait_recv()

    shift = shifts[h]
    lane24 = lane_iota((I_LOC, 128))
    poly_f = poly_row.astype(F32)

    def build(k, c):
        zz, hh = lax.rem(k, 4), lax.div(k, 4)
        row = pl.multiple_of(k * I_LOC, 8)
        own = fac[pl.ds(row, I_LOC), :]
        t = [br[q * 4 + zz, hh].astype(F32) for q in range(4)]
        tiles = [
            t[0][:, :128],
            jnp.where(lane24 < 64, t[0][:, 128:], t[1][:, :128]),
            t[1][:, 128:],
            t[2][:, :128],
            jnp.where(lane24 < 64, t[2][:, 128:], t[3][:, :128]),
            t[3][:, 128:],
        ]
        for n in range(6):
            cols = slice(n * 128, (n + 1) * 128)
            full = tiles[n] + jnp.where(own != poly_f[:, cols], shift, F32(0.0))
            full = jnp.where(amino_row[:, cols] > 0, full * F32(LOG2E), F32(-1e9))
            bias[pl.ds(row, I_LOC), cols] = full
        return c

    lax.fori_loop(0, N_RES, build, 0)

    lane_q = lane_iota((Q_CHUNK, 128))
    lane = lane_iota((RES, 128))
    for half in range(2):
        pltpu.make_async_copy(recv.at[half], recv.at[half], rs.at[half]).wait()
        qs[...] = recv[half, :, 0].astype(F32).reshape(RES, 128).astype(BF16)
        kf = recv[half, :, 1].astype(F32).reshape(RES, 128)
        for n in range(6):
            rows = slice(n * 128, (n + 1) * 128)
            ks[rows, :] = jnp.where(amino_col[n] > 0, kf[rows], F32(0.0)).astype(BF16)
        vs[...] = recv[half, :, 2].astype(F32).reshape(RES, 128).astype(BF16)

        def one_row(rr, c, half=half):
            slot = in_slot(lane, rr)
            xv = jnp.where(slot, vs[...].astype(F32), F32(1.0)).astype(BF16)
            xk = ks[...]
            slot_q = in_slot(lane_q, rr)
            for q0 in range(0, RES, Q_CHUNK):
                rows = slice(q0, q0 + Q_CHUNK)
                xq = jnp.where(slot_q, qs[rows, :].astype(F32), F32(0.0)).astype(BF16)
                sc = nt_dot(xq, xk) + bias[rows, :]
                m = jnp.max(sc, axis=-1, keepdims=True)
                p = jnp.exp2(sc - m).astype(BF16)
                o = jnp.dot(p, xv, preferred_element_type=F32)
                o = o / pltpu.roll(o, 32, 1)
                acc[half, rows, :] = jnp.where(slot_q, o, acc[half, rows, :])
            return c

        lax.fori_loop(0, 4, one_row, 0)
        ret[half] = acc[half].reshape(N_RES, I_LOC, 128).astype(BF16)
        pltpu.make_async_copy(ret.at[half, r], back.at[half, r], rb.at[half]).start()

        def send_back(k, c, half=half):
            d = offset(k, r)
            remote(ret.at[half, d], back.at[half, r], sb.at[half], rb.at[half], d, s).start()
            return c

        lax.fori_loop(1, N_RES, send_back, 0)

    def yz(k):
        kk = lax.rem(k * 3, 8)
        return lax.div(kk, 4), lax.rem(kk, 4)

    def send_left(half):
        pltpu.make_async_copy(lbuf.at[half], lall.at[s, half], rl).start()

        def send(k, c):
            q = lax.rem(s + k, 4)
            remote(lbuf.at[half], lall.at[s, half], sl, rl, r, q).start()
            return c

        lax.fori_loop(1, N_SEQ, send, 0)

    def send_right(half):
        blk = lax.rem(r, 8)

        @pl.when(holds)
        def _():
            pltpu.make_async_copy(rbuf.at[half], rall.at[blk, s, half], rr_sem.at[blk]).start()

        def send(k, c):
            dy, dz = yz(lax.div(k, 4))
            x = lax.rem(b + k, 4)
            d = x * 8 + lax.rem(y_lo + dy, 2) * 4 + lax.rem(z + dz, 4)

            @pl.when(jnp.logical_or(k != 0, jnp.logical_not(holds)))
            def _():
                remote(rbuf.at[half], rall.at[blk, s, half], sr, rr_sem.at[blk], d, b).start()

            return c

        lax.fori_loop(0, N_RES, send, 0)

    lane16 = lane_iota((16, 128))
    for n in range(6):
        tr[n * 128 : (n + 1) * 128, :] = amino_col[n]
    own_live = tr[pl.ds(pl.multiple_of(r * I_LOC, 8), I_LOC), :]
    for half in range(2):
        pltpu.make_async_copy(back.at[half], back.at[half], rb.at[half]).wait()
        gated = jnp.concatenate(
            [
                (back[half, 4 * hh : 4 * hh + 4].astype(F32) * gate[half, hh]).reshape(4 * I_LOC, 128)
                for hh in range(HEADS)
            ],
            axis=1,
        ).astype(BF16)
        for k in range(4):
            delta = jnp.dot(
                gated, bd_mix[:, k * CM : (k + 1) * CM], preferred_element_type=F32
            ).reshape(4, I_LOC, CM)
            fams = []
            for g in range(4):
                row = g * 8 + half * 4 + k
                fam = msa[row] + live[s * S_LOC + row].astype(F32) * delta[g]
                family[row] = fam
                fams.append(fam)
            y = layer_norm(jnp.concatenate(fams, axis=0)).astype(BF16)
            f = nt_dot(y, wfac_t[...])
            f = jnp.concatenate([f, jnp.zeros((4 * I_LOC, 64), F32)], axis=1)
            for g in range(4):
                on = live[s * S_LOC + g * 8 + half * 4 + k].astype(F32)
                at = (g * 4 + k) * I_LOC
                fac[at : at + I_LOC, :] = f[g * I_LOC : (g + 1) * I_LOC] * (on * own_live)
        for i0 in range(0, I_LOC, 4):
            tile = None
            for k in range(4):
                i = i0 + k
                f = fac[pl.ds(i, 16, stride=I_LOC), :]
                moved = pltpu.roll(f, k * 32, 1) if k else f
                tile = moved if tile is None else jnp.where(in_slot(lane16, k), moved, tile)
                ft = jnp.transpose(f, (1, 0))[OPM : 2 * OPM, :]
                tr[i * OPM : (i + 1) * OPM, :] = jnp.concatenate(
                    [ft, jnp.zeros((OPM, 112), F32)], axis=1
                )
            lbuf[half, :, i0 * 32 : (i0 + 4) * 32] = tile.astype(BF16)
        send_left(half)
        for e0 in range(0, OPM, 8):
            tile = tr[pl.ds(e0, I_LOC, stride=OPM), :]
            for k in range(1, 8):
                moved = pltpu.roll(tr[pl.ds(e0 + k, I_LOC, stride=OPM), :], k * 16, 1)
                tile = jnp.where(lane24 >= k * 16, moved, tile)
            rbuf[half, :, e0 * 16 : (e0 + 8) * 16] = tile.astype(BF16)
        send_right(half)

    pltpu.make_async_copy(lall, lall, rl).wait()
    left = lall[...].reshape(N_SEQ * S_LOC, I_LOC * OPM)
    for n in range(6):
        lw[n] = left[:, n * 128 : (n + 1) * 128]
    count = lax.fori_loop(0, 128, lambda k, c: c + live[k], jnp.int32(0)).astype(F32)
    inv = 1.0 / jnp.maximum(jnp.full((1, 128), count, F32), 1.0)

    for c0 in range(0, 8, J_BLOCKS):
        blocks = []
        for t in range(J_BLOCKS):
            dy, dz = yz(c0 + t)
            blocks.append(lax.rem(y_lo + 2 - dy, 2) * 4 + lax.rem(z + 4 - dz, 4))
        for blk in blocks:
            pltpu.make_async_copy(rall.at[blk], rall.at[blk], rr_sem.at[blk]).wait()
        for ge in range(4):
            cols = slice(ge * 128, (ge + 1) * 128)
            tiles = [
                jnp.concatenate([rall[blk, q, half, :, cols].astype(F32) for blk in blocks], axis=0)
                for q in range(N_SEQ)
                for half in range(2)
            ]
            for e, tile in enumerate(exchange_lanes(tiles, 16)):
                lhs[(ge * 8 + e) * JC : (ge * 8 + e + 1) * JC, :] = tile.astype(BF16)

        def spread(p, c):
            w2 = jnp.concatenate([lw[2 * p], lw[2 * p + 1]], axis=1)
            o = jnp.dot(lhs[...], w2, preferred_element_type=F32).astype(BF16)
            for t in range(2):
                for g in range(8):
                    tiles = [
                        o[(4 * g + k) * JC : (4 * g + k + 1) * JC, t * 128 : (t + 1) * 128]
                        for k in range(4)
                    ]
                    for m, tile in enumerate(exchange_lanes(tiles, 32)):
                        amat[(2 * p + t) * 4 + m, :, g * 128 : (g + 1) * 128] = tile
            return c

        lax.fori_loop(0, 3, spread, 0)

        def finish(p, c, blocks=tuple(blocks)):
            am = amat[pl.ds(12 * p, 12)].reshape(12 * JC, 1024)
            o = jnp.dot(am, tcat[...], preferred_element_type=F32)
            o = ((o[:, :128] + o[:, 128:]) * inv).reshape(12, JC, CZ)
            for t, blk in enumerate(blocks):
                at = (pl.ds(12 * p, 12), pl.ds(pl.multiple_of(blk * I_LOC, 8), I_LOC))
                contact[at] = pair[at] + o[:, t * I_LOC : (t + 1) * I_LOC]
            return c

        lax.fori_loop(0, I_LOC // 12, finish, 0)

    remote(bsend.at[pl.ds(0, 7)], b1.at[pl.ds(0, 7)], s1, r1, r, s_c).wait_send()
    remote(br.at[pl.ds(0, 8)], br.at[pl.ds(0, 8)], s3, r3, r, s_c).wait_send()
    remote(qsend.at[pl.ds(0, 31)], qsend.at[pl.ds(0, 31)], ss, r3, r, s_c).wait_send()
    for half in range(2):
        remote(
            ret.at[half, pl.ds(0, 31)], ret.at[half, pl.ds(0, 31)], sb.at[half], r3, r, s_c
        ).wait_send()
    remote(lall.at[pl.ds(0, 3)], lall.at[pl.ds(0, 3)], sl, r3, r, s_c).wait_send()
    remote(rall.at[pl.ds(0, 7)], rall.at[pl.ds(0, 7)], sr, r3, r, s_c).wait_send()
    last = rall.at[7, pl.ds(0, 3)]
    remote(last, last, sr, r3, r, s_c).wait_send()

    @pl.when(jnp.logical_not(holds))
    def _():
        rest = rall.at[7, 3]
        remote(rest, rest, sr, r3, r, s_c).wait_send()


def on_device(msa, pair, amino, poly, live, w, wshift, shifts, wmix, wfac, tmat):
    dma = pltpu.SemaphoreType.DMA
    vm = pl.BlockSpec(memory_space=pltpu.VMEM)
    sm = pl.BlockSpec(memory_space=pltpu.SMEM)
    return pl.pallas_call(
        kernel,
        out_shape=(
            jax.ShapeDtypeStruct((S_LOC, I_LOC, CM), F32),
            jax.ShapeDtypeStruct((I_LOC, J_LOC, CZ), F32),
        ),
        in_specs=[vm] * 9 + [sm] * 2,
        out_specs=(vm, vm),
        scratch_shapes=[
            pltpu.VMEM((2, I_LOC * HEADS, 128), F32),
            pltpu.VMEM((HEADS, I_LOC, 256), BF16),
            pltpu.VMEM((HEADS, I_LOC, 256), BF16),
            pltpu.VMEM((N_SEQ * 4, HEADS, I_LOC, 256), BF16),
            pltpu.VMEM((RES, RES), F32),
            pltpu.VMEM((RES, CM), F32),
            pltpu.VMEM((2, HEADS, 4, I_LOC, 128), F32),
            pltpu.VMEM((N_RES, 2, 3, I_LOC, 128), BF16),
            pltpu.VMEM((2, N_RES, 3, I_LOC, 128), BF16),
            pltpu.VMEM((RES, 128), BF16),
            pltpu.VMEM((RES, 128), BF16),
            pltpu.VMEM((RES, 128), BF16),
            pltpu.VMEM((2, RES, 128), F32),
            pltpu.VMEM((2, N_RES, I_LOC, 128), BF16),
            pltpu.VMEM((2, N_RES, I_LOC, 128), BF16),
            pltpu.VMEM((1024, 1024), BF16),
            pltpu.VMEM((S_LOC * I_LOC, 128), F32),
            pltpu.VMEM((I_LOC * OPM, 128), F32),
            pltpu.VMEM((2, 16, I_LOC * OPM), BF16),
            pltpu.VMEM((2, I_LOC, OPM * 16), BF16),
            pltpu.VMEM((N_SEQ, 2, 16, I_LOC * OPM), BF16),
            pltpu.VMEM((8, N_SEQ, 2, I_LOC, OPM * 16), BF16),
            pltpu.VMEM((6, N_SEQ * S_LOC, 128), BF16),
            pltpu.VMEM((1024, 256), BF16),
            pltpu.VMEM((OPM * JC, 128), BF16),
            pltpu.VMEM((I_LOC, JC, 1024), BF16),
            dma, dma((2,)), dma, dma, dma, dma((8,)), dma, dma,
            dma((2,)), dma((2,)), dma, dma, dma, dma((8,)), dma((1,)),
        ],
        compiler_params=pltpu.CompilerParams(
            collective_id=0, has_side_effects=True, vmem_limit_bytes=VMEM_LIMIT
        ),
        name="evoformer",
    )(msa, pair, amino, poly, w, wshift.T, wmix, wfac.T, tmat, live, shifts)


def solution(mesh):
    in_specs = (P("seq", "res", None), P("res", "seq", None)) + (P(),) * 9
    out_specs = (P("seq", "res", None), P("res", "seq", None))
    return jax.shard_map(
        on_device, mesh=mesh, in_specs=in_specs, out_specs=out_specs, check_vma=False
    )
```

time: 114 us -> 93.1 us (0.82)
  the two profiles are of different devices: /device:TPU:5 before, /device:TPU:0 now
where the time goes in v3:
time: 93.1 us; the launch traced here: 91.4 us
  Pallas kernels  85.4 us (92%)
  local copies, waits for them, and re-layouts  5.36 us (6%)
    pallas_call x1, Pallas kernels, on_device(): pl.pallas_call(kernel, out_shape=(jax.ShapeDtypeStruct((S_LOC, I_LOC, CM)...  85.4 us
    unnamed x2, local copies, waits for them, and re-layouts  5.36 us

profile of v3, /device:TPU:0, one launch (start us, length us, event | category | flops | bytes accessed | tf_op | source)
XLA Modules:
  0.0 91.4 jit_solution(4112829504018445106)
XLA Ops:
  0.6 85.4 %evoformer.1 = (f32[32,24,256]{2,1,0:T(8,128)}, f32[24,192,128]{2,1,0:T(8,128)}) custom-call(f32[32,24,256]{2,1,0:T(8,128)} %msa.1, f32[24,192,128]{2,1,0:T(8,128)} %pair.1, s32[768]{0:T(1024)} %amino.1, s32[768]{0:T(1024)} %poly.1, bf16[256,1024]{1,0:T(8,128)(2,1)} %w.1, f32[8,128]{1,0:T(8,128)} %bitcast.3, bf16[256,256]{1,0:T(8,128)(2,1)} %wmix.1, ...), custom_call_target="tpu_custom_call" | custom-call | tf_op jit(solution)/shard_map/evoformer/pallas_call | solution.py:468
  86.0 2.1 %copy.15 = f32[32,24,256]{2,1,0:T(8,128)} copy(f32[32,24,256]{2,1,0:T(8,128)} %get-tuple-element.4) | data formatting | bytes 1572864
  88.1 3.3 %copy.16 = f32[24,192,128]{2,1,0:T(8,128)} copy(f32[24,192,128]{2,1,0:T(8,128)} %get-tuple-element.5) | data formatting | bytes 4718592

commit v4 on v3

v4 whole, which is shorter than its diff:
```python
import math

import jax
import jax.numpy as jnp
from jax import lax
from jax.experimental import pallas as pl
from jax.experimental.pallas import tpu as pltpu
from jax.sharding import PartitionSpec as P

MESH = pl.DeviceIdType.MESH
F32 = jnp.float32
BF16 = jnp.bfloat16
LOG2E = math.log2(math.e)
VMEM_LIMIT = 58 * 1024 * 1024

N_RES, N_SEQ = 32, 4
S_LOC, I_LOC, J_LOC = 32, 24, 192
CM, CZ, HEADS, HD, OPM = 256, 128, 8, 32, 32
RES = 768
Q_CHUNK, K_CHUNK = 384, 256
OFFSETS = [((k * 11) % 32 // 8, (k * 11) % 8 // 4, (k * 11) % 4) for k in range(1, N_RES)]
YZ = [((k * 3) % 8 // 4, (k * 3) % 4) for k in range(8)]
J_BLOCKS = 2
JC = J_BLOCKS * I_LOC


def lane_iota(shape):
    return lax.broadcasted_iota(jnp.int32, shape, len(shape) - 1)


def in_slot(lane, k):
    return (lane >= k * 32) & (lane < (k + 1) * 32)


def layer_norm(x):
    centre = jnp.mean(x, axis=-1, keepdims=True)
    d = x - centre
    spread = jnp.mean(d * d, axis=-1, keepdims=True)
    return d * lax.rsqrt(spread + 1e-05)


def nt_dot(a, b, precision=None):
    return lax.dot_general(
        a, b, (((1,), (1,)), ((), ())), precision=precision, preferred_element_type=F32
    )


def exchange_lanes(tiles, width):
    lane = lane_iota(tiles[0].shape)
    tiles, bit = list(tiles), 1
    while bit < len(tiles):
        low = lax.rem(lane, 2 * bit * width) < bit * width
        new = list(tiles)
        for k in range(len(tiles)):
            if not k & bit:
                a, b = tiles[k], tiles[k | bit]
                new[k] = jnp.where(low, a, pltpu.roll(b, bit * width, 1))
                new[k | bit] = jnp.where(low, pltpu.roll(a, 128 - bit * width, 1), b)
        tiles, bit = new, 2 * bit
    return tiles


def remote(src, dst, a, b, d, q):
    return pltpu.make_async_remote_copy(
        src_ref=src, dst_ref=dst, send_sem=a, recv_sem=b, device_id=(d, q), device_id_type=MESH
    )


def kernel(
    msa_hbm, pair_hbm, w_hbm, wmix_hbm, tmat_hbm, amino, poly, wshift_t, wfac_t, live, shifts,
    delta_hbm, proj_hbm,
    msa, pair, w, wmix, tmat, dbuf, pbuf,
    btmp, bsend, b1, b2, br, bias, pgate, gate, qsend, recv, qs, ks, vs, acc, ret, back,
    wrep, wfac, fac, tr, lbuf, rbuf, lall, rall, lw, tcat, lhs, amat,
    ss, rs, s1, r1, s2, r2, s3, r3, sb, rb, sl, rl, sr, rr_sem, loc, ins, outs,
):
    r, s = lax.axis_index("res"), lax.axis_index("seq")
    h, z = lax.div(r, 4), lax.rem(r, 4)
    y_lo, b = lax.rem(h, 2), lax.div(r, 8)
    s_c = s + 1 - 2 * lax.rem(s, 2)
    holds = b == s
    xs = [lax.rem(b + k, 4) * 8 for k in range(4)]
    ys = [lax.rem(y_lo + k, 2) * 4 for k in range(2)]
    zs = [lax.rem(z + k, 4) for k in range(4)]
    seqs = [lax.rem(s + k, 4) for k in range(4)]
    partners = [xs[i] + ys[j] + zs[k] for i, j, k in OFFSETS]

    loads = [
        pltpu.make_async_copy(src, dst, ins.at[6 + n])
        for n, (src, dst) in enumerate(
            ((msa_hbm, msa), (w_hbm, w), (wmix_hbm, wmix), (tmat_hbm, tmat))
        )
    ]
    pair_loads = [
        pltpu.make_async_copy(pair_hbm.at[pl.ds(4 * n, 4)], pair.at[pl.ds(4 * n, 4)], ins.at[n])
        for n in range(6)
    ]
    for cp in loads[:2] + pair_loads + loads[2:]:
        cp.start()

    barrier = pltpu.get_barrier_semaphore()

    def greet(d, q):
        pl.semaphore_signal(barrier, inc=1, device_id=(d, q), device_id_type=MESH)

    for d in partners:
        greet(d, s)
    for k in range(4):
        greet(h * 4 + k, seqs[2])
    for k in range(1, N_SEQ):
        greet(r, seqs[k])
    for dy, dz in YZ:
        for k in range(N_SEQ):
            if dy or dz or k:
                greet(8 * s + ys[dy] + zs[dz], seqs[k])

    @pl.when(jnp.logical_not(holds))
    def _():
        greet(8 * s + ys[0] + zs[0], s)

    loads[0].wait()
    loads[1].wait()
    normed = layer_norm(msa[...].reshape(S_LOC * I_LOC, CM)).astype(BF16)
    lane3 = lane_iota((8, I_LOC, 128))
    for part in range(3):
        out = jnp.dot(normed, w[:, part * CM : (part + 1) * CM], preferred_element_type=F32)
        if part == 0:
            out = out * F32(LOG2E / math.sqrt(HD))
        for t in range(2):
            cols = out[:, t * 128 : (t + 1) * 128].reshape(8, 4, I_LOC, 128)
            for a in range(4):
                tile = None
                for k in range(4):
                    piece = cols[:, k]
                    if (k - a) % 4:
                        piece = pltpu.roll(piece, (k - a) % 4 * 32, 2)
                    tile = piece if tile is None else jnp.where(in_slot(lane3, k), piece, tile)
                tile = tile.astype(BF16)
                for g in range(4):
                    for half in range(2):
                        qsend[(t * 4 + a) * 4 + g, half, part] = tile[g * 2 + half]

    btmp[...] = jnp.zeros_like(btmp)
    chunk = 4
    for i0 in range(0, I_LOC, chunk):
        pair_loads[i0 // chunk].wait()
        zn = layer_norm(pair[i0 : i0 + chunk].reshape(chunk * J_LOC, CZ))
        bb = nt_dot(wshift_t[...], zn, lax.Precision.HIGHEST)
        for i in range(chunk):
            rows, col = slice((i0 + i) * HEADS, (i0 + i + 1) * HEADS), i * J_LOC
            btmp[0, rows, :] = bb[:, col : col + 128]
            btmp[1, rows, 0:64] = bb[:, col + 128 : col + J_LOC]
    odd = jnp.full((I_LOC, 128), lax.rem(s, 2), jnp.int32) > 0
    swap = jnp.full((I_LOC, 128), lax.rem(h, 2), jnp.int32) > 0
    lane24 = lane_iota((I_LOC, 128))
    low24 = lane24 < 64
    for hh in range(HEADS):
        v0, v1 = (btmp[n, pl.ds(hh, I_LOC, stride=HEADS), :] for n in range(2))
        t0, t1 = pltpu.roll(v0, 64, 1), pltpu.roll(v1, 64, 1)
        bsend[hh, 0] = jnp.where(odd, jnp.where(low24, t0, t1), v0).astype(BF16)
        part = jnp.where(odd, v0, v1)
        bsend[hh, 1] = jnp.where(swap, pltpu.roll(part, 64, 1), part).astype(BF16)

    pl.semaphore_wait(barrier, 31 + 4 + 3 + N_RES - holds.astype(jnp.int32))

    def send_rows(half):
        pltpu.make_async_copy(qsend.at[r, half], recv.at[half, r], rs.at[half]).start()
        for d in partners:
            remote(qsend.at[d, half], recv.at[half, r], ss, rs.at[half], d, s).start()

    pltpu.make_async_copy(bsend.at[h], b1.at[h], r1).start()
    for i in range(4):
        for j in range(2):
            if i or j:
                d = xs[i] + ys[j] + z
                remote(bsend.at[lax.div(d, 4)], b1.at[h], s1, r1, d, s).start()

    send_rows(0)

    pgate[...] = jnp.dot(normed, w[:, 3 * CM :], preferred_element_type=F32).astype(BF16).astype(F32)
    for t in range(2):
        cols = jax.nn.sigmoid(pgate[:, t * 128 : (t + 1) * 128]).reshape(8, 4, I_LOC, 128)
        for a in range(4):
            tile = None
            for k in range(4):
                piece = cols[:, k]
                if (k - a) % 4:
                    piece = pltpu.roll(piece, (k - a) % 4 * 32, 2)
                tile = piece if tile is None else jnp.where(in_slot(lane3, k), piece, tile)
            for g in range(4):
                for half in range(2):
                    gate[half, t * 4 + a, g] = tile[g * 2 + half]

    pltpu.make_async_copy(bsend, b1, r1).wait()
    for k in range(HEADS):
        b2[k] = b1[k, 0]
    for k in range(4):
        b2[8 + k] = jnp.where(
            low24, b1[2 * k, 1].astype(F32), b1[2 * k + 1, 1].astype(F32)
        ).astype(BF16)
    slot = s * 4 + z
    mine2 = lax.div(s, 2) * 4 + z
    own2 = pltpu.make_async_copy(b2, br.at[slot], loc.at[0])
    own2.start()
    for k in range(1, 8):
        zz, q = zs[k // 2], seqs[k % 2 * 2]
        remote(b2, br.at[slot], s2, r2.at[mine2], h * 4 + zz, q).start()
    remote(b2, br.at[slot], s3, r3.at[z], r, s_c).start()

    loads[2].wait()
    loads[3].wait()
    for hh in range(HEADS):
        for k in range(4):
            wrep[hh * 128 + k * 32 : hh * 128 + (k + 1) * 32, :] = wmix[hh * HD : (hh + 1) * HD, :]
    wfac[...] = jnp.concatenate([wfac_t[...], jnp.zeros((64, CM), BF16)], axis=0)
    for e in range(OPM):
        t = tmat[pl.ds(e, OPM, stride=OPM), :]
        head = t.astype(BF16)
        tcat[e * 32 : (e + 1) * 32, 0:128] = head
        tcat[e * 32 : (e + 1) * 32, 128:256] = (t - head.astype(F32)).astype(BF16)
    acc[...] = jnp.zeros_like(acc)
    amino_row = amino[...].reshape(1, RES)
    poly_row = poly[...].reshape(1, RES)

    def column(row, n):
        tile = row[:, n * 128 : (n + 1) * 128].astype(F32)
        return jnp.transpose(jnp.broadcast_to(tile, (128, 128)), (1, 0))

    amino_col = [column(amino_row, n) for n in range(6)]
    for n in range(6):
        fac[n * 128 : (n + 1) * 128, :] = column(poly_row, n)

    remote(br.at[pl.ds(0, 7)], br.at[pl.ds(0, 7)], s2, r1, r, s_c).wait_send()
    send_rows(1)

    shift = shifts[h]
    poly_f = poly_row.astype(F32)

    def build(zz, pair_n):
        for parity in range(2):
            hh = 2 * pair_n + parity
            row = pl.multiple_of((hh * 4 + zz) * I_LOC, 8)
            own = fac[pl.ds(row, I_LOC), :]
            full = [br[q * 4 + zz, hh].astype(F32) for q in range(4)]
            part = [br[q * 4 + zz, 8 + pair_n].astype(F32) for q in range(4)]
            for q in range(4):
                if q % 2 != parity:
                    part[q] = pltpu.roll(part[q], 64, 1)
            tiles = [
                full[0], jnp.where(low24, part[0], part[1]), full[1],
                full[2], jnp.where(low24, part[2], part[3]), full[3],
            ]
            for n in range(6):
                cols = slice(n * 128, (n + 1) * 128)
                val = tiles[n] + jnp.where(own != poly_f[:, cols], shift, F32(0.0))
                val = jnp.where(amino_row[:, cols] > 0, val * F32(LOG2E), F32(-1e9))
                bias[pl.ds(row, I_LOC), cols] = val

    def finish_z(zz):
        remote(br.at[pl.ds(0, 2)], br.at[pl.ds(0, 2)], s3, r3.at[zz], r, s_c).wait_recv()

        def step(pair_n, c):
            build(zz, pair_n)
            return c

        lax.fori_loop(0, 4, step, 0)

    own2.wait()
    before = None
    for k in (0, 3, 2, 1):
        for y in range(2):
            if k or y:
                zz, q = zs[k], seqs[2 * y]
                at = q * 4 + zz
                remote(
                    b2, br.at[at], s2, r2.at[lax.div(q, 2) * 4 + zz], h * 4 + zz, q
                ).wait_recv()
                remote(br.at[at], br.at[at], s3, r3.at[zz], r, s_c).start()
        if before is not None:
            finish_z(before)
        before = zs[k]
    finish_z(before)

    lane_q = lane_iota((Q_CHUNK, 128))
    lane = lane_iota((RES, 128))
    for half in range(2):
        pltpu.make_async_copy(recv.at[half], recv.at[half], rs.at[half]).wait()
        qs[...] = recv[half, :, 0].astype(F32).reshape(RES, 128).astype(BF16)
        kf = recv[half, :, 1].astype(F32).reshape(RES, 128)
        for n in range(6):
            rows = slice(n * 128, (n + 1) * 128)
            ks[rows, :] = jnp.where(amino_col[n] > 0, kf[rows], F32(0.0)).astype(BF16)
        vs[...] = recv[half, :, 2].astype(F32).reshape(RES, 128).astype(BF16)

        def one_row(rr):
            slot = in_slot(lane, rr)
            xv = jnp.where(slot, vs[...].astype(F32), F32(1.0)).astype(BF16)
            xk = ks[...]
            slot_q = in_slot(lane_q, rr)
            for q0 in range(0, RES, Q_CHUNK):
                rows = slice(q0, q0 + Q_CHUNK)
                xq = jnp.where(slot_q, qs[rows, :].astype(F32), F32(0.0)).astype(BF16)
                o = m = None
                for k0 in range(0, RES, K_CHUNK):
                    keys = slice(k0, k0 + K_CHUNK)
                    sc = nt_dot(xq, xk[keys]) + bias[rows, keys]
                    m1 = jnp.max(sc, axis=-1, keepdims=True)
                    p = jnp.exp2(sc - m1).astype(BF16)
                    o1 = jnp.dot(p, xv[keys], preferred_element_type=F32)
                    if o is None:
                        o, m = o1, m1
                    else:
                        top = jnp.maximum(m, m1)
                        o = o * jnp.exp2(m - top) + o1 * jnp.exp2(m1 - top)
                        m = top
                o = o / pltpu.roll(o, 32, 1)
                acc[half, rows, :] = jnp.where(slot_q, o, acc[half, rows, :])

        def two_rows(rr, c):
            one_row(2 * rr)
            one_row(2 * rr + 1)
            return c

        lax.fori_loop(0, 2, two_rows, 0)
        ret[half] = acc[half].reshape(N_RES, I_LOC, 128).astype(BF16)
        pltpu.make_async_copy(ret.at[half, r], back.at[half, r], rb.at[half]).start()

        for d in partners:
            remote(ret.at[half, d], back.at[half, r], sb.at[half], rb.at[half], d, s).start()

    def send_left(half):
        pltpu.make_async_copy(lbuf.at[half], lall.at[s, half], rl).start()
        for k in range(1, N_SEQ):
            remote(lbuf.at[half], lall.at[s, half], sl, rl, r, seqs[k]).start()

    blk_r = lax.rem(r, 8)

    def send_right(half, k):
        dy, dz = YZ[k // 4]
        cp = remote(
            rbuf.at[half], rall.at[blk_r, s, half], sr, rr_sem.at[blk_r], xs[k % 4] + ys[dy] + zs[dz], b
        )
        if k:
            cp.start()
        else:

            @pl.when(holds)
            def _():
                pltpu.make_async_copy(rbuf.at[half], rall.at[blk_r, s, half], rr_sem.at[blk_r]).start()

            @pl.when(jnp.logical_not(holds))
            def _():
                cp.start()

    lane16 = lane_iota((16, 128))
    lane96 = lane_iota((4 * I_LOC, 128))
    for n in range(6):
        tr[n * 128 : (n + 1) * 128, :] = amino_col[n]
    own_live = tr[pl.ds(pl.multiple_of(r * I_LOC, 8), I_LOC), :]
    for half in range(2):
        pltpu.make_async_copy(back.at[half], back.at[half], rb.at[half]).wait()
        heads = [
            (back[half, 4 * hh : 4 * hh + 4].astype(F32) * gate[half, hh]).reshape(4 * I_LOC, 128)
            for hh in range(HEADS)
        ]
        gated = jnp.concatenate(
            [
                jnp.concatenate(
                    [jnp.where(in_slot(lane96, k), t, F32(0.0)).astype(BF16) for t in heads], axis=1
                )
                for k in range(4)
            ],
            axis=0,
        )
        delta = jnp.dot(gated, wrep[...], preferred_element_type=F32).reshape(16, I_LOC, CM)
        fams = []
        for k in range(4):
            for g in range(4):
                row = g * 8 + half * 4 + k
                step = live[s * S_LOC + row].astype(F32) * delta[k * 4 + g]
                dbuf[row] = step
                fams.append(msa[row] + step)
        y = layer_norm(jnp.concatenate(fams, axis=0)).astype(BF16)
        f = nt_dot(y, wfac[...])
        for k in range(4):
            for g in range(4):
                on = live[s * S_LOC + g * 8 + half * 4 + k].astype(F32)
                at = (k * 4 + g) * I_LOC
                fac[at : at + I_LOC, :] = f[at : at + I_LOC] * (on * own_live)
        for i0 in range(0, I_LOC, 4):
            tile = None
            for k in range(4):
                i = i0 + k
                f = fac[pl.ds(i, 16, stride=I_LOC), :]
                moved = pltpu.roll(f, k * 32, 1) if k else f
                tile = moved if tile is None else jnp.where(in_slot(lane16, k), moved, tile)
                ft = jnp.transpose(f, (1, 0))[OPM : 2 * OPM, :]
                tr[i * OPM : (i + 1) * OPM, :] = jnp.concatenate(
                    [ft, jnp.zeros((OPM, 112), F32)], axis=1
                )
            lbuf[half, :, i0 * 32 : (i0 + 4) * 32] = tile.astype(BF16)
        send_left(half)
        for e0 in range(0, OPM, 8):
            tile = tr[pl.ds(e0, I_LOC, stride=OPM), :]
            for k in range(1, 8):
                moved = pltpu.roll(tr[pl.ds(e0 + k, I_LOC, stride=OPM), :], k * 16, 1)
                tile = jnp.where(lane24 >= k * 16, moved, tile)
            rbuf[half, :, e0 * 16 : (e0 + 8) * 16] = tile.astype(BF16)
        if half == 0:
            for k in range(16):
                send_right(0, k)
        else:
            for k in range(16):
                send_right(1, k)
            for k in range(16, N_RES):
                send_right(0, k)
                send_right(1, k)
            out_delta = pltpu.make_async_copy(dbuf, delta_hbm, outs.at[16])
            out_delta.start()

    def take_left():
        pltpu.make_async_copy(lall, lall, rl).wait()
        left = lall[...].reshape(N_SEQ * S_LOC, I_LOC * OPM)
        for n in range(6):
            lw[n] = left[:, n * 128 : (n + 1) * 128]

    count = lax.fori_loop(0, 128, lambda k, c: c + live[k], jnp.int32(0)).astype(F32)
    inv = 1.0 / jnp.maximum(jnp.full((1, 128), count, F32), 1.0)

    out_proj = []
    for c0 in range(0, 8, J_BLOCKS):
        blocks = []
        for t in range(J_BLOCKS):
            dy, dz = YZ[c0 + t]
            blocks.append(ys[dy] + zs[(4 - dz) % 4])
        for blk in blocks:
            pltpu.make_async_copy(rall.at[blk], rall.at[blk], rr_sem.at[blk]).wait()
        for ge in range(4):
            cols = slice(ge * 128, (ge + 1) * 128)
            tiles = [
                jnp.concatenate([rall[blk, q, half, :, cols].astype(F32) for blk in blocks], axis=0)
                for q in range(N_SEQ)
                for half in range(2)
            ]
            for e, tile in enumerate(exchange_lanes(tiles, 16)):
                lhs[(ge * 8 + e) * JC : (ge * 8 + e + 1) * JC, :] = tile.astype(BF16)
        if c0 == 0:
            take_left()

        def spread(p, c):
            w2 = jnp.concatenate([lw[2 * p], lw[2 * p + 1]], axis=1)
            o = jnp.dot(lhs[...], w2, preferred_element_type=F32).astype(BF16)
            for t in range(2):
                for g in range(8):
                    tiles = [
                        o[(4 * g + k) * JC : (4 * g + k + 1) * JC, t * 128 : (t + 1) * 128]
                        for k in range(4)
                    ]
                    for m, tile in enumerate(exchange_lanes(tiles, 32)):
                        amat[(2 * p + t) * 4 + m, :, g * 128 : (g + 1) * 128] = tile
            return c

        lax.fori_loop(0, 3, spread, 0)

        for p in range(2):
            some = pl.ds(12 * p, 12)
            o = jnp.dot(amat[some].reshape(12 * JC, 1024), tcat[...], preferred_element_type=F32)
            o = ((o[:, :128] + o[:, 128:]) * inv).reshape(12, JC, CZ)
            for t, blk in enumerate(blocks):
                pbuf[blk, some] = o[:, t * I_LOC : (t + 1) * I_LOC]
                out = pltpu.make_async_copy(
                    pbuf.at[blk, some],
                    proj_hbm.at[some, pl.ds(pl.multiple_of(blk * I_LOC, 8), I_LOC)],
                    outs.at[2 * (c0 + t) + p],
                )
                out.start()
                out_proj.append(out)

    out_delta.wait()
    for out in out_proj:
        out.wait()
    remote(bsend.at[pl.ds(0, 7)], b1.at[pl.ds(0, 7)], s1, r1, r, s_c).wait_send()
    remote(br.at[pl.ds(0, 8)], br.at[pl.ds(0, 8)], s3, r1, r, s_c).wait_send()
    remote(qsend.at[pl.ds(0, 31)], qsend.at[pl.ds(0, 31)], ss, r1, r, s_c).wait_send()
    for half in range(2):
        remote(
            ret.at[half, pl.ds(0, 31)], ret.at[half, pl.ds(0, 31)], sb.at[half], r1, r, s_c
        ).wait_send()
    remote(lall.at[pl.ds(0, 3)], lall.at[pl.ds(0, 3)], sl, r1, r, s_c).wait_send()
    remote(rall.at[pl.ds(0, 7)], rall.at[pl.ds(0, 7)], sr, r1, r, s_c).wait_send()
    last = rall.at[7, pl.ds(0, 3)]
    remote(last, last, sr, r1, r, s_c).wait_send()

    @pl.when(jnp.logical_not(holds))
    def _():
        rest = rall.at[7, 3]
        remote(rest, rest, sr, r1, r, s_c).wait_send()


def on_device(msa, pair, amino, poly, live, w, wshift, shifts, wmix, wfac, tmat):
    dma = pltpu.SemaphoreType.DMA
    vm = pl.BlockSpec(memory_space=pltpu.VMEM)
    sm = pl.BlockSpec(memory_space=pltpu.SMEM)
    hbm = pl.BlockSpec(memory_space=pl.ANY)
    delta, proj = pl.pallas_call(
        kernel,
        out_shape=(
            jax.ShapeDtypeStruct((S_LOC, I_LOC, CM), F32),
            jax.ShapeDtypeStruct((I_LOC, J_LOC, CZ), F32),
        ),
        in_specs=[hbm] * 5 + [vm] * 4 + [sm] * 2,
        out_specs=(hbm, hbm),
        scratch_shapes=[
            pltpu.VMEM((S_LOC, I_LOC, CM), F32),
            pltpu.VMEM((I_LOC, J_LOC, CZ), F32),
            pltpu.VMEM((CM, 4 * CM), BF16),
            pltpu.VMEM((CM, CM), BF16),
            pltpu.VMEM((OPM * OPM, CZ), F32),
            pltpu.VMEM((S_LOC, I_LOC, CM), F32),
            pltpu.VMEM((8, I_LOC, I_LOC, CZ), F32),
            pltpu.VMEM((2, I_LOC * HEADS, 128), F32),
            pltpu.VMEM((HEADS, 2, I_LOC, 128), BF16),
            pltpu.VMEM((HEADS, 2, I_LOC, 128), BF16),
            pltpu.VMEM((12, I_LOC, 128), BF16),
            pltpu.VMEM((N_SEQ * 4, 12, I_LOC, 128), BF16),
            pltpu.VMEM((RES, RES), F32),
            pltpu.VMEM((RES, CM), F32),
            pltpu.VMEM((2, HEADS, 4, I_LOC, 128), F32),
            pltpu.VMEM((N_RES, 2, 3, I_LOC, 128), BF16),
            pltpu.VMEM((2, N_RES, 3, I_LOC, 128), BF16),
            pltpu.VMEM((RES, 128), BF16),
            pltpu.VMEM((RES, 128), BF16),
            pltpu.VMEM((RES, 128), BF16),
            pltpu.VMEM((2, RES, 128), F32),
            pltpu.VMEM((2, N_RES, I_LOC, 128), BF16),
            pltpu.VMEM((2, N_RES, I_LOC, 128), BF16),
            pltpu.VMEM((1024, CM), BF16),
            pltpu.VMEM((128, CM), BF16),
            pltpu.VMEM((RES, 128), F32),
            pltpu.VMEM((I_LOC * OPM, 128), F32),
            pltpu.VMEM((2, 16, I_LOC * OPM), BF16),
            pltpu.VMEM((2, I_LOC, OPM * 16), BF16),
            pltpu.VMEM((N_SEQ, 2, 16, I_LOC * OPM), BF16),
            pltpu.VMEM((8, N_SEQ, 2, I_LOC, OPM * 16), BF16),
            pltpu.VMEM((6, N_SEQ * S_LOC, 128), BF16),
            pltpu.VMEM((1024, 256), BF16),
            pltpu.VMEM((OPM * JC, 128), BF16),
            pltpu.VMEM((I_LOC, JC, 1024), BF16),
            dma, dma((2,)), dma, dma, dma, dma((8,)), dma, dma((4,)),
            dma((2,)), dma((2,)), dma, dma, dma, dma((8,)), dma((1,)),
            dma((10,)), dma((17,)),
        ],
        compiler_params=pltpu.CompilerParams(
            collective_id=0, has_side_effects=True, vmem_limit_bytes=VMEM_LIMIT
        ),
        name="evoformer",
    )(msa, pair, w, wmix, tmat, amino, poly, wshift.T, wfac.T, live, shifts)
    return msa + delta, pair + proj


def solution(mesh):
    in_specs = (P("seq", "res", None), P("res", "seq", None)) + (P(),) * 9
    out_specs = (P("seq", "res", None), P("res", "seq", None))
    return jax.shard_map(
        on_device, mesh=mesh, in_specs=in_specs, out_specs=out_specs, check_vma=False
    )
```

time: 93.1 us -> 84 us (0.902); the launches traced: 91.4 us -> 83.9 us
  Pallas kernels: 85.4 us -> 79.1 us
  local copies, waits for them, and re-layouts: 5.36 us -> 0.01 us
  other arithmetic: 0 us -> 4.03 us
    pallas_call x1, Pallas kernels: 85.4 us -> 79.1 us  [on_device(): pl.pallas_call(kernel, out_shape=(jax.ShapeDtypeStruct((S_LOC, I_LOC, CM)...]
    unnamed x2 -> x6, local copies, waits for them, and re-layouts: 5.36 us -> 0.01 us
    add x0 -> x2, other arithmetic: none -> 4.03 us  [on_device(): return (msa + delta, pair + proj)]
where the time goes in v4:
time: 84 us; the launch traced here: 83.9 us
  Pallas kernels  79.1 us (94%)
  other arithmetic  4.03 us (5%)
    pallas_call x1, Pallas kernels, on_device(): pl.pallas_call(kernel, out_shape=(jax.ShapeDtypeStruct((S_LOC, I_LOC, CM)...  79.1 us
    add x2, other arithmetic, on_device(): return (msa + delta, pair + proj)  4.03 us

profile of v4, /device:TPU:0, one launch (start us, length us, event | category | flops | bytes accessed | tf_op | source)
XLA Modules:
  0.0 83.9 jit_solution(6040801659911366001)
XLA Ops:
  0.6 0.0 copy-start.1
  0.6 0.0 copy-start
  0.7 79.1 %evoformer.1 = (f32[32,24,256]{2,1,0:T(8,128)}, f32[24,192,128]{2,1,0:T(8,128)}) custom-call(f32[32,24,256]{2,1,0:T(8,128)} %msa_hbm.1, f32[24,192,128]{2,1,0:T(8,128)} %pair_hbm.1, bf16[256,1024]{1,0:T(8,128)(2,1)} %w_hbm.1, bf16[256,256]{1,0:T(8,128)(2,1)} %wmix_hbm.1, f32[1024,128]{1,0:T(8,128)} %tmat_hbm.1, s32[768]{0:T(1024)} %amino.1, s32[768]{0:T(1024)} %poly.1, ...), custom_call_target="tpu_custom_call" | custom-call | tf_op jit(solution)/shard_map/evoformer/pallas_call | solution.py:505
  79.8 0.0 copy-start.2
  79.8 0.0 copy-done.1
  79.8 2.3 %add.6 = f32[32,24,256]{2,1,0:T(8,128)} add(f32[32,24,256]{2,1,0:T(8,128)S(1)} %copy-done.1, f32[32,24,256]{2,1,0:T(8,128)} %get-tuple-element.4) | non-fusion elementwise | flops 196608 | bytes 2359296 | tf_op jit(solution)/shard_map/add | solution.py:558
  82.1 0.0 copy-done
  82.1 0.0 copy-done.2
  82.1 1.8 %add.7 = f32[24,192,128]{2,1,0:T(8,128)} add(f32[24,192,128]{2,1,0:T(8,128)S(1)} %copy-done, f32[24,192,128]{2,1,0:T(8,128)S(1)} %copy-done.2) | non-fusion elementwise | flops 589824 | bytes 7077888 | tf_op jit(solution)/shard_map/add | solution.py:558
Async XLA Ops:
  0.6 79.2 %copy-start.1 = (f32[32,24,256]{2,1,0:T(8,128)S(1)}, f32[32,24,256]{2,1,0:T(8,128)}, u32[]{:S(2)}) copy-start(f32[32,24,256]{2,1,0:T(8,128)} %msa_hbm.1) | copy-start | bytes 2359300
  0.6 81.4 %copy-start = (f32[24,192,128]{2,1,0:T(8,128)S(1)}, f32[24,192,128]{2,1,0:T(8,128)}, u32[]{:S(2)}) copy-start(f32[24,192,128]{2,1,0:T(8,128)} %pair_hbm.1) | copy-start | bytes 7077892
  79.8 2.3 %copy-start.2 = (f32[24,192,128]{2,1,0:T(8,128)S(1)}, f32[24,192,128]{2,1,0:T(8,128)}, u32[]{:S(2)}) copy-start(f32[24,192,128]{2,1,0:T(8,128)} %get-tuple-element.5) | copy-start | bytes 7077892

commit v5 on v4

--- a/solution.py
+++ b/solution.py
@@ -71,14 +71,13 @@
     delta_hbm, proj_hbm,
     msa, pair, w, wmix, tmat, dbuf, pbuf,
     btmp, bsend, b1, b2, br, bias, pgate, gate, qsend, recv, qs, ks, vs, acc, ret, back,
-    wrep, wfac, fac, tr, lbuf, rbuf, lall, rall, lw, tcat, lhs, amat,
-    ss, rs, s1, r1, s2, r2, s3, r3, sb, rb, sl, rl, sr, rr_sem, loc, ins, outs,
+    wrep, wfac, fac, tr, lbuf, xbuf, lall, rall, lw, tcat, lhs, amat,
+    ss, rs, s1, r1, s2, r2, s3, r3, sb, rb, sl, rl, sx, rx, sr, rr_sem, loc, ins, outs,
 ):
     r, s = lax.axis_index("res"), lax.axis_index("seq")
     h, z = lax.div(r, 4), lax.rem(r, 4)
     y_lo, b = lax.rem(h, 2), lax.div(r, 8)
     s_c = s + 1 - 2 * lax.rem(s, 2)
-    holds = b == s
     xs = [lax.rem(b + k, 4) * 8 for k in range(4)]
     ys = [lax.rem(y_lo + k, 2) * 4 for k in range(2)]
     zs = [lax.rem(z + k, 4) for k in range(4)]
@@ -112,11 +111,7 @@
     for dy, dz in YZ:
         for k in range(N_SEQ):
             if dy or dz or k:
-                greet(8 * s + ys[dy] + zs[dz], seqs[k])
-
-    @pl.when(jnp.logical_not(holds))
-    def _():
-        greet(8 * s + ys[0] + zs[0], s)
+                greet(8 * b + ys[dy] + zs[dz], seqs[k])
 
     loads[0].wait()
     loads[1].wait()
@@ -142,8 +137,9 @@
 
     btmp[...] = jnp.zeros_like(btmp)
     chunk = 4
+    for cp in pair_loads:
+        cp.wait()
     for i0 in range(0, I_LOC, chunk):
-        pair_loads[i0 // chunk].wait()
         zn = layer_norm(pair[i0 : i0 + chunk].reshape(chunk * J_LOC, CZ))
         bb = nt_dot(wshift_t[...], zn, lax.Precision.HIGHEST)
         for i in range(chunk):
@@ -161,12 +157,14 @@
         part = jnp.where(odd, v0, v1)
         bsend[hh, 1] = jnp.where(swap, pltpu.roll(part, 64, 1), part).astype(BF16)
 
-    pl.semaphore_wait(barrier, 31 + 4 + 3 + N_RES - holds.astype(jnp.int32))
-
-    def send_rows(half):
+    pl.semaphore_wait(barrier, 31 + 4 + 3 + 31)
+
+    def send_rows(half, some):
+        for d in some:
+            remote(qsend.at[d, half], recv.at[half, r], ss, rs.at[half], d, s).start()
+
+    for half in range(2):
         pltpu.make_async_copy(qsend.at[r, half], recv.at[half, r], rs.at[half]).start()
-        for d in partners:
-            remote(qsend.at[d, half], recv.at[half, r], ss, rs.at[half], d, s).start()
 
     pltpu.make_async_copy(bsend.at[h], b1.at[h], r1).start()
     for i in range(4):
@@ -175,7 +173,7 @@
                 d = xs[i] + ys[j] + z
                 remote(bsend.at[lax.div(d, 4)], b1.at[h], s1, r1, d, s).start()
 
-    send_rows(0)
+    send_rows(0, partners)
 
     pgate[...] = jnp.dot(normed, w[:, 3 * CM :], preferred_element_type=F32).astype(BF16).astype(F32)
     for t in range(2):
@@ -231,7 +229,7 @@
         fac[n * 128 : (n + 1) * 128, :] = column(poly_row, n)
 
     remote(br.at[pl.ds(0, 7)], br.at[pl.ds(0, 7)], s2, r1, r, s_c).wait_send()
-    send_rows(1)
+    send_rows(1, partners)
 
     shift = shifts[h]
     poly_f = poly_row.astype(F32)
@@ -335,22 +333,23 @@
 
     blk_r = lax.rem(r, 8)
 
-    def send_right(half, k):
+    def send_x(half):
+        block = xbuf.at[half, b]
+        for k in range(1, 4):
+            remote(block, block, sx.at[half], rx.at[half], xs[k] + ys[0] + zs[0], s).start()
+
+    def wait_x(half):
+        three = xbuf.at[half, pl.ds(0, 3)]
+        remote(three, three, sx.at[half], rx.at[half], r, s_c).wait_recv()
+
+    def send_right(half, k, group):
         dy, dz = YZ[k // 4]
-        cp = remote(
-            rbuf.at[half], rall.at[blk_r, s, half], sr, rr_sem.at[blk_r], xs[k % 4] + ys[dy] + zs[dz], b
-        )
+        x = seqs[k % 4]
+        src, dst, sem = xbuf.at[half, x], rall.at[blk_r, s, half], rr_sem.at[blk_r]
         if k:
-            cp.start()
+            remote(src, dst, sr.at[group], sem, 8 * b + ys[dy] + zs[dz], x).start()
         else:
-
-            @pl.when(holds)
-            def _():
-                pltpu.make_async_copy(rbuf.at[half], rall.at[blk_r, s, half], rr_sem.at[blk_r]).start()
-
-            @pl.when(jnp.logical_not(holds))
-            def _():
-                cp.start()
+            pltpu.make_async_copy(src, dst, sem).start()
 
     lane16 = lane_iota((16, 128))
     lane96 = lane_iota((4 * I_LOC, 128))
@@ -405,16 +404,15 @@
             for k in range(1, 8):
                 moved = pltpu.roll(tr[pl.ds(e0 + k, I_LOC, stride=OPM), :], k * 16, 1)
                 tile = jnp.where(lane24 >= k * 16, moved, tile)
-            rbuf[half, :, e0 * 16 : (e0 + 8) * 16] = tile.astype(BF16)
+            xbuf[half, b, :, e0 * 16 : (e0 + 8) * 16] = tile.astype(BF16)
+        send_x(half)
+        wait_x(half)
         if half == 0:
             for k in range(16):
-                send_right(0, k)
+                send_right(0, k, 4)
         else:
-            for k in range(16):
-                send_right(1, k)
-            for k in range(16, N_RES):
-                send_right(0, k)
-                send_right(1, k)
+            for k in range(8):
+                send_right(1, k, 0)
             out_delta = pltpu.make_async_copy(dbuf, delta_hbm, outs.at[16])
             out_delta.start()
 
@@ -424,15 +422,44 @@
         for n in range(6):
             lw[n] = left[:, n * 128 : (n + 1) * 128]
 
+    def wait_sent(group, blocks):
+        for size, ref in ((8, rall.at[0]), (2, rall.at[0, 0]), (1, rall.at[0, 0, 0])):
+            for _ in range(blocks // size):
+                remote(ref, ref, sr.at[group], r1, r, s_c).wait_send()
+            blocks %= size
+
+    def send_group(group):
+        for k in range(8 * group, 8 * group + 8):
+            send_right(0, k, group)
+            send_right(1, k, group)
+
     count = lax.fori_loop(0, 128, lambda k, c: c + live[k], jnp.int32(0)).astype(F32)
     inv = 1.0 / jnp.maximum(jnp.full((1, 128), count, F32), 1.0)
 
-    out_proj = []
-    for c0 in range(0, 8, J_BLOCKS):
+    wait_sent(0, 7)
+    for k in range(8, 16):
+        send_right(1, k, 1)
+    send_group(2)
+
+    def blocks_of(c):
         blocks = []
         for t in range(J_BLOCKS):
-            dy, dz = YZ[c0 + t]
-            blocks.append(ys[dy] + zs[(4 - dz) % 4])
+            kk = lax.rem((c * J_BLOCKS + t) * 3, 8)
+            blocks.append(
+                lax.rem(y_lo + 2 - lax.div(kk, 4), 2) * 4 + lax.rem(z + 4 - lax.rem(kk, 4), 4)
+            )
+        return blocks
+
+    def result(c, t, p, blk):
+        some = pl.ds(12 * p, 12)
+        return pltpu.make_async_copy(
+            pbuf.at[blk, some],
+            proj_hbm.at[some, pl.ds(pl.multiple_of(blk * I_LOC, 8), I_LOC)],
+            outs.at[c * 4 + t * 2 + p],
+        )
+
+    def one_chunk(c, carry):
+        blocks = blocks_of(c)
         for blk in blocks:
             pltpu.make_async_copy(rall.at[blk], rall.at[blk], rr_sem.at[blk]).wait()
         for ge in range(4):
@@ -444,10 +471,14 @@
             ]
             for e, tile in enumerate(exchange_lanes(tiles, 16)):
                 lhs[(ge * 8 + e) * JC : (ge * 8 + e + 1) * JC, :] = tile.astype(BF16)
-        if c0 == 0:
+
+        @pl.when(c == 0)
+        def _():
+            wait_sent(1, 8)
+            send_group(3)
             take_left()
 
-        def spread(p, c):
+        def spread(p, cc):
             w2 = jnp.concatenate([lw[2 * p], lw[2 * p + 1]], axis=1)
             o = jnp.dot(lhs[...], w2, preferred_element_type=F32).astype(BF16)
             for t in range(2):
@@ -458,27 +489,33 @@
                     ]
                     for m, tile in enumerate(exchange_lanes(tiles, 32)):
                         amat[(2 * p + t) * 4 + m, :, g * 128 : (g + 1) * 128] = tile
-            return c
+            return cc
 
         lax.fori_loop(0, 3, spread, 0)
 
-        for p in range(2):
+        def finish(p, cc):
             some = pl.ds(12 * p, 12)
             o = jnp.dot(amat[some].reshape(12 * JC, 1024), tcat[...], preferred_element_type=F32)
             o = ((o[:, :128] + o[:, 128:]) * inv).reshape(12, JC, CZ)
             for t, blk in enumerate(blocks):
                 pbuf[blk, some] = o[:, t * I_LOC : (t + 1) * I_LOC]
-                out = pltpu.make_async_copy(
-                    pbuf.at[blk, some],
-                    proj_hbm.at[some, pl.ds(pl.multiple_of(blk * I_LOC, 8), I_LOC)],
-                    outs.at[2 * (c0 + t) + p],
-                )
-                out.start()
-                out_proj.append(out)
+                result(c, t, p, blk).start()
+            return cc
+
+        lax.fori_loop(0, 2, finish, 0)
+        return carry
+
+    lax.fori_loop(0, 8 // J_BLOCKS, one_chunk, 0)
 
     out_delta.wait()
-    for out in out_proj:
-        out.wait()
+
+    def result_out(c, carry):
+        for t, blk in enumerate(blocks_of(c)):
+            for p in range(2):
+                result(c, t, p, blk).wait()
+        return carry
+
+    lax.fori_loop(0, 8 // J_BLOCKS, result_out, 0)
     remote(bsend.at[pl.ds(0, 7)], b1.at[pl.ds(0, 7)], s1, r1, r, s_c).wait_send()
     remote(br.at[pl.ds(0, 8)], br.at[pl.ds(0, 8)], s3, r1, r, s_c).wait_send()
     remote(qsend.at[pl.ds(0, 31)], qsend.at[pl.ds(0, 31)], ss, r1, r, s_c).wait_send()
@@ -487,14 +524,12 @@
             ret.at[half, pl.ds(0, 31)], ret.at[half, pl.ds(0, 31)], sb.at[half], r1, r, s_c
         ).wait_send()
     remote(lall.at[pl.ds(0, 3)], lall.at[pl.ds(0, 3)], sl, r1, r, s_c).wait_send()
-    remote(rall.at[pl.ds(0, 7)], rall.at[pl.ds(0, 7)], sr, r1, r, s_c).wait_send()
-    last = rall.at[7, pl.ds(0, 3)]
-    remote(last, last, sr, r1, r, s_c).wait_send()
-
-    @pl.when(jnp.logical_not(holds))
-    def _():
-        rest = rall.at[7, 3]
-        remote(rest, rest, sr, r1, r, s_c).wait_send()
+    wait_sent(2, 16)
+    wait_sent(3, 16)
+    wait_sent(4, 15)
+    for half in range(2):
+        three = xbuf.at[half, pl.ds(0, 3)]
+        remote(three, three, sx.at[half], r1, r, s_c).wait_send()
 
 
 def on_device(msa, pair, amino, poly, live, w, wshift, shifts, wmix, wfac, tmat):
@@ -539,7 +574,7 @@
             pltpu.VMEM((RES, 128), F32),
             pltpu.VMEM((I_LOC * OPM, 128), F32),
             pltpu.VMEM((2, 16, I_LOC * OPM), BF16),
-            pltpu.VMEM((2, I_LOC, OPM * 16), BF16),
+            pltpu.VMEM((2, 4, I_LOC, OPM * 16), BF16),
             pltpu.VMEM((N_SEQ, 2, 16, I_LOC * OPM), BF16),
             pltpu.VMEM((8, N_SEQ, 2, I_LOC, OPM * 16), BF16),
             pltpu.VMEM((6, N_SEQ * S_LOC, 128), BF16),
@@ -547,7 +582,8 @@
             pltpu.VMEM((OPM * JC, 128), BF16),
             pltpu.VMEM((I_LOC, JC, 1024), BF16),
             dma, dma((2,)), dma, dma, dma, dma((8,)), dma, dma((4,)),
-            dma((2,)), dma((2,)), dma, dma, dma, dma((8,)), dma((1,)),
+            dma((2,)), dma((2,)), dma, dma, dma((2,)), dma((2,)),
+            dma((5,)), dma((8,)), dma((1,)),
             dma((10,)), dma((17,)),
         ],
         compiler_params=pltpu.CompilerParams(

time: 84 us -> 80.9 us (0.963)
  the two profiles are of different devices: /device:TPU:0 before, /device:TPU:1 now
where the time goes in v5:
time: 80.9 us; the launch traced here: 80.7 us
  Pallas kernels  76 us (94%)
  other arithmetic  4.03 us (5%)
    pallas_call x1, Pallas kernels, on_device(): pl.pallas_call(kernel, out_shape=(jax.ShapeDtypeStruct((S_LOC, I_LOC, CM)...  76 us
    add x2, other arithmetic, on_device(): return (msa + delta, pair + proj)  4.03 us

profile of v5, /device:TPU:1, one launch (start us, length us, event | category | flops | bytes accessed | tf_op | source)
XLA Modules:
  0.0 80.7 jit_solution(369364482199354894)
XLA Ops:
  0.6 0.0 copy-start.1
  0.6 0.0 copy-start
  0.7 76.0 %evoformer.1 = (f32[32,24,256]{2,1,0:T(8,128)}, f32[24,192,128]{2,1,0:T(8,128)}) custom-call(f32[32,24,256]{2,1,0:T(8,128)} %msa_hbm.1, f32[24,192,128]{2,1,0:T(8,128)} %pair_hbm.1, bf16[256,1024]{1,0:T(8,128)(2,1)} %w_hbm.1, bf16[256,256]{1,0:T(8,128)(2,1)} %wmix_hbm.1, f32[1024,128]{1,0:T(8,128)} %tmat_hbm.1, s32[768]{0:T(1024)} %amino.1, s32[768]{0:T(1024)} %poly.1, ...), custom_call_target="tpu_custom_call" | custom-call | tf_op jit(solution)/shard_map/evoformer/pallas_call | solution.py:540
  76.7 0.0 copy-start.2
  76.7 0.0 copy-done.1
  76.7 2.3 %add.6 = f32[32,24,256]{2,1,0:T(8,128)} add(f32[32,24,256]{2,1,0:T(8,128)S(1)} %copy-done.1, f32[32,24,256]{2,1,0:T(8,128)} %get-tuple-element.4) | non-fusion elementwise | flops 196608 | bytes 2359296 | tf_op jit(solution)/shard_map/add | solution.py:594
  79.0 0.0 copy-done
  79.0 0.0 copy-done.2
  79.0 1.8 %add.7 = f32[24,192,128]{2,1,0:T(8,128)} add(f32[24,192,128]{2,1,0:T(8,128)S(1)} %copy-done, f32[24,192,128]{2,1,0:T(8,128)S(1)} %copy-done.2) | non-fusion elementwise | flops 589824 | bytes 7077888 | tf_op jit(solution)/shard_map/add | solution.py:594
Async XLA Ops:
  0.6 76.1 %copy-start.1 = (f32[32,24,256]{2,1,0:T(8,128)S(1)}, f32[32,24,256]{2,1,0:T(8,128)}, u32[]{:S(2)}) copy-start(f32[32,24,256]{2,1,0:T(8,128)} %msa_hbm.1) | copy-start | bytes 2359300
  0.6 78.3 %copy-start = (f32[24,192,128]{2,1,0:T(8,128)S(1)}, f32[24,192,128]{2,1,0:T(8,128)}, u32[]{:S(2)}) copy-start(f32[24,192,128]{2,1,0:T(8,128)} %pair_hbm.1) | copy-start | bytes 7077892
  76.7 2.3 %copy-start.2 = (f32[24,192,128]{2,1,0:T(8,128)S(1)}, f32[24,192,128]{2,1,0:T(8,128)}, u32[]{:S(2)}) copy-start(f32[24,192,128]{2,1,0:T(8,128)} %get-tuple-element.5) | copy-start | bytes 7077892

commit v6 on v5

--- a/solution.py
+++ b/solution.py
@@ -436,10 +436,8 @@
     count = lax.fori_loop(0, 128, lambda k, c: c + live[k], jnp.int32(0)).astype(F32)
     inv = 1.0 / jnp.maximum(jnp.full((1, 128), count, F32), 1.0)
 
-    wait_sent(0, 7)
     for k in range(8, 16):
         send_right(1, k, 1)
-    send_group(2)
 
     def blocks_of(c):
         blocks = []
@@ -474,9 +472,12 @@
 
         @pl.when(c == 0)
         def _():
-            wait_sent(1, 8)
+            send_group(2)
+            take_left()
+
+        @pl.when(c == 1)
+        def _():
             send_group(3)
-            take_left()
 
         def spread(p, cc):
             w2 = jnp.concatenate([lw[2 * p], lw[2 * p + 1]], axis=1)
@@ -524,6 +525,8 @@
             ret.at[half, pl.ds(0, 31)], ret.at[half, pl.ds(0, 31)], sb.at[half], r1, r, s_c
         ).wait_send()
     remote(lall.at[pl.ds(0, 3)], lall.at[pl.ds(0, 3)], sl, r1, r, s_c).wait_send()
+    wait_sent(0, 7)
+    wait_sent(1, 8)
     wait_sent(2, 16)
     wait_sent(3, 16)
     wait_sent(4, 15)

time: 80.9 us -> 83.3 us (1.030)
  the two profiles are of different devices: /device:TPU:1 before, /device:TPU:0 now
where the time goes in v6:
time: 83.3 us; the launch traced here: 81.8 us
  Pallas kernels  77.1 us (93%)
  other arithmetic  4.03 us (5%)
    pallas_call x1, Pallas kernels, on_device(): pl.pallas_call(kernel, out_shape=(jax.ShapeDtypeStruct((S_LOC, I_LOC, CM)...  77.1 us
    add x2, other arithmetic, on_device(): return (msa + delta, pair + proj)  4.03 us

profile of v6, /device:TPU:0, one launch (start us, length us, event | category | flops | bytes accessed | tf_op | source)
XLA Modules:
  0.0 81.8 jit_solution(13395559317645230953)
XLA Ops:
  0.6 0.0 copy-start.1
  0.6 0.0 copy-start
  0.7 77.1 %evoformer.1 = (f32[32,24,256]{2,1,0:T(8,128)}, f32[24,192,128]{2,1,0:T(8,128)}) custom-call(f32[32,24,256]{2,1,0:T(8,128)} %msa_hbm.1, f32[24,192,128]{2,1,0:T(8,128)} %pair_hbm.1, bf16[256,1024]{1,0:T(8,128)(2,1)} %w_hbm.1, bf16[256,256]{1,0:T(8,128)(2,1)} %wmix_hbm.1, f32[1024,128]{1,0:T(8,128)} %tmat_hbm.1, s32[768]{0:T(1024)} %amino.1, s32[768]{0:T(1024)} %poly.1, ...), custom_call_target="tpu_custom_call" | custom-call | tf_op jit(solution)/shard_map/evoformer/pallas_call | solution.py:543
  77.8 0.0 copy-start.2
  77.8 0.0 copy-done.1
  77.8 2.3 %add.6 = f32[32,24,256]{2,1,0:T(8,128)} add(f32[32,24,256]{2,1,0:T(8,128)S(1)} %copy-done.1, f32[32,24,256]{2,1,0:T(8,128)} %get-tuple-element.4) | non-fusion elementwise | flops 196608 | bytes 2359296 | tf_op jit(solution)/shard_map/add | solution.py:597
  80.1 0.0 copy-done
  80.1 0.0 copy-done.2
  80.1 1.8 %add.7 = f32[24,192,128]{2,1,0:T(8,128)} add(f32[24,192,128]{2,1,0:T(8,128)S(1)} %copy-done, f32[24,192,128]{2,1,0:T(8,128)S(1)} %copy-done.2) | non-fusion elementwise | flops 589824 | bytes 7077888 | tf_op jit(solution)/shard_map/add | solution.py:597
Async XLA Ops:
  0.6 77.1 %copy-start.1 = (f32[32,24,256]{2,1,0:T(8,128)S(1)}, f32[32,24,256]{2,1,0:T(8,128)}, u32[]{:S(2)}) copy-start(f32[32,24,256]{2,1,0:T(8,128)} %msa_hbm.1) | copy-start | bytes 2359300
  0.6 79.4 %copy-start = (f32[24,192,128]{2,1,0:T(8,128)S(1)}, f32[24,192,128]{2,1,0:T(8,128)}, u32[]{:S(2)}) copy-start(f32[24,192,128]{2,1,0:T(8,128)} %pair_hbm.1) | copy-start | bytes 7077892
  77.8 2.3 %copy-start.2 = (f32[24,192,128]{2,1,0:T(8,128)S(1)}, f32[24,192,128]{2,1,0:T(8,128)}, u32[]{:S(2)}) copy-start(f32[24,192,128]{2,1,0:T(8,128)} %get-tuple-element.5) | copy-start | bytes 7077892

commit v7 on v5

--- a/solution.py
+++ b/solution.py
@@ -173,7 +173,7 @@
                 d = xs[i] + ys[j] + z
                 remote(bsend.at[lax.div(d, 4)], b1.at[h], s1, r1, d, s).start()
 
-    send_rows(0, partners)
+    send_rows(0, partners[:16])
 
     pgate[...] = jnp.dot(normed, w[:, 3 * CM :], preferred_element_type=F32).astype(BF16).astype(F32)
     for t in range(2):
@@ -204,6 +204,7 @@
         zz, q = zs[k // 2], seqs[k % 2 * 2]
         remote(b2, br.at[slot], s2, r2.at[mine2], h * 4 + zz, q).start()
     remote(b2, br.at[slot], s3, r3.at[z], r, s_c).start()
+    send_rows(0, partners[16:])
 
     loads[2].wait()
     loads[3].wait()

time: 80.9 us -> 84.3 us (1.042)
  the two profiles are of different devices: /device:TPU:1 before, /device:TPU:0 now
where the time goes in v7:
time: 84.3 us; the launch traced here: 83.3 us
  Pallas kernels  78.6 us (93%)
  other arithmetic  4.03 us (5%)
    pallas_call x1, Pallas kernels, on_device(): pl.pallas_call(kernel, out_shape=(jax.ShapeDtypeStruct((S_LOC, I_LOC, CM)...  78.6 us
    add x2, other arithmetic, on_device(): return (msa + delta, pair + proj)  4.03 us

profile of v7, /device:TPU:0, one launch (start us, length us, event | category | flops | bytes accessed | tf_op | source)
XLA Modules:
  0.0 83.3 jit_solution(17442035251930796551)
XLA Ops:
  0.6 0.0 copy-start.1
  0.6 0.0 copy-start
  0.7 78.6 %evoformer.1 = (f32[32,24,256]{2,1,0:T(8,128)}, f32[24,192,128]{2,1,0:T(8,128)}) custom-call(f32[32,24,256]{2,1,0:T(8,128)} %msa_hbm.1, f32[24,192,128]{2,1,0:T(8,128)} %pair_hbm.1, bf16[256,1024]{1,0:T(8,128)(2,1)} %w_hbm.1, bf16[256,256]{1,0:T(8,128)(2,1)} %wmix_hbm.1, f32[1024,128]{1,0:T(8,128)} %tmat_hbm.1, s32[768]{0:T(1024)} %amino.1, s32[768]{0:T(1024)} %poly.1, ...), custom_call_target="tpu_custom_call" | custom-call | tf_op jit(solution)/shard_map/evoformer/pallas_call | solution.py:541
  79.2 0.0 copy-start.2
  79.2 0.0 copy-done.1
  79.3 2.3 %add.6 = f32[32,24,256]{2,1,0:T(8,128)} add(f32[32,24,256]{2,1,0:T(8,128)S(1)} %copy-done.1, f32[32,24,256]{2,1,0:T(8,128)} %get-tuple-element.4) | non-fusion elementwise | flops 196608 | bytes 2359296 | tf_op jit(solution)/shard_map/add | solution.py:595
  81.5 0.0 copy-done
  81.5 0.0 copy-done.2
  81.5 1.8 %add.7 = f32[24,192,128]{2,1,0:T(8,128)} add(f32[24,192,128]{2,1,0:T(8,128)S(1)} %copy-done, f32[24,192,128]{2,1,0:T(8,128)S(1)} %copy-done.2) | non-fusion elementwise | flops 589824 | bytes 7077888 | tf_op jit(solution)/shard_map/add | solution.py:595
Async XLA Ops:
  0.6 78.6 %copy-start.1 = (f32[32,24,256]{2,1,0:T(8,128)S(1)}, f32[32,24,256]{2,1,0:T(8,128)}, u32[]{:S(2)}) copy-start(f32[32,24,256]{2,1,0:T(8,128)} %msa_hbm.1) | copy-start | bytes 2359300
  0.6 80.9 %copy-start = (f32[24,192,128]{2,1,0:T(8,128)S(1)}, f32[24,192,128]{2,1,0:T(8,128)}, u32[]{:S(2)}) copy-start(f32[24,192,128]{2,1,0:T(8,128)} %pair_hbm.1) | copy-start | bytes 7077892
  79.2 2.3 %copy-start.2 = (f32[24,192,128]{2,1,0:T(8,128)S(1)}, f32[24,192,128]{2,1,0:T(8,128)}, u32[]{:S(2)}) copy-start(f32[24,192,128]{2,1,0:T(8,128)} %get-tuple-element.5) | copy-start | bytes 7077892
